TPU v7x, 32 devices: a whole 2x2x4 slice. The times are simulated.
32 devices in a mesh: seq: 8 (over z, y), head: 4 (over x, core).
Axes of the slice: x: 2, y: 2, z: 4, core: 2. Of those that a mesh axis runs over, the one named last changes fastest.
Arguments:
- query: bfloat16 [5120, 2048], P(('seq', 'head')), may hold values from -5 to 5
- key: bfloat16 [5120, 2048], P(('seq', 'head')), may hold values from -5 to 5
- value: bfloat16 [5120, 2048], P(('seq', 'head')), may hold values from -6 to 6
- grad_out: bfloat16 [5120, 2048], P(('seq', 'head')), may hold values from -6 to 6
- rand_blocks: int32 [80, 3], replicated, may hold values from 0 to 79, as said below
Outputs:
- grad_query: bfloat16 [5120, 2048], P(('seq', 'head'))
- grad_key: bfloat16 [5120, 2048], P(('seq', 'head'))
- grad_value: bfloat16 [5120, 2048], P(('seq', 'head'))
Inputs may be any that keep to these rules, and one draw needn't show every extreme that they name: `rand_blocks`: row j lists the 3 random key blocks of query block j. Block b lies on index b // 10 of seq. The blocks of one row lie on 3 different indices. No listed block lies on index 0 or on the index of the query block itself. The query blocks of one index of seq list at most 5 blocks lying on any one other index.
All inputs are finite; a program needn't handle non-finite values.
Results may differ from a plain program's by a relative error of at most 0.008.
Values may be sent and summed in bfloat16 or wider, within the bound.
A program may use at most 384 MiB of HBM per device.

v0:
```python
import jax
import jax.numpy as jnp
from jax import lax
from jax.sharding import PartitionSpec as P

HD = 128
BLOCK = 64
G = 2
R = 3


big_negative = -1e30


def broadcast(block, axis, source):
    block = jnp.where(lax.axis_index(axis) == source, block, jnp.zeros_like(block))
    return lax.psum(block, axis)


def extended_2(shard, sides, width):
    for axis, dim in sides:
        peers, length = (lax.axis_size(axis), shard.shape[dim])
        up = [(i, (i + 1) % peers) for i in range(peers - 1)]
        down = [(j, i) for i, j in up]
        last = lax.slice_in_dim(shard, length - width, length, axis=dim)
        leading = lax.slice_in_dim(shard, 0, width, axis=dim)
        before = lax.ppermute(last, axis, up)
        after = lax.ppermute(leading, axis, down)
        shard = jnp.concatenate([before, shard, after], axis=dim)
    return shard


def request_plan(requested, device, per_dev):
    wanted_row = requested[device]
    owners = wanted_row // per_dev
    within = wanted_row % per_dev
    usable = jnp.ones(wanted_row.shape, jnp.bool_)
    positions = jnp.arange(owners.shape[0])
    earlier = (owners[:, None] == owners[None, :]) & (positions[None, :] < positions[:, None])
    slot_rank = jnp.sum(earlier.astype(jnp.int32), axis=1)
    return (owners, within, slot_rank, usable)


def on_device(query, key, value, grad_out, rand_blocks):
    queries, keys, values, out_grads = (
        lax.all_to_all(query, "head", split_axis=1, concat_axis=0, tiled=True),
        lax.all_to_all(key, "head", split_axis=1, concat_axis=0, tiled=True),
        lax.all_to_all(value, "head", split_axis=1, concat_axis=0, tiled=True),
        lax.all_to_all(grad_out, "head", split_axis=1, concat_axis=0, tiled=True),
    )
    tokens, features = queries.shape
    head_count = features // HD
    per_dev = tokens // BLOCK
    seq_count = lax.axis_size("seq")
    device = lax.axis_index("seq")
    capacity = (per_dev * R + seq_count - 3) // (seq_count - 2)
    rand_count = per_dev * R
    slots_total = 3 + G + R
    score_scale = HD ** (-0.5)
    requested = rand_blocks.reshape(seq_count, rand_count)
    owners_all, within_all, rank_all, usable_all = jax.vmap(
        lambda sender: request_plan(requested, sender, per_dev)
    )(jnp.arange(seq_count, dtype=jnp.int32))
    to_me = usable_all & (owners_all == device)
    slot_ids = jnp.arange(capacity)
    block_ids = jnp.arange(per_dev)
    matches = (
        to_me[:, :, None, None]
        & (rank_all[:, :, None, None] == slot_ids[None, None, :, None])
        & (within_all[:, :, None, None] == block_ids[None, None, None, :])
    )
    chooser = jnp.sum(matches.astype(jnp.float32), axis=1)
    my_owners, my_within, my_rank, my_usable = request_plan(requested, device, per_dev)
    my_slot = jnp.clip(my_owners, 0, seq_count - 1) * capacity + my_rank
    own_pairs = jnp.stack([keys, values]).reshape(2, per_dev, BLOCK, features)
    served = None
    served = jnp.einsum(
        "dcb,sbxf->dcsxf",
        chooser.astype(jnp.bfloat16),
        own_pairs,
        preferred_element_type=jnp.float32,
    ).astype(jnp.bfloat16)
    outgoing = served.reshape(seq_count * capacity, 2, BLOCK, features)
    incoming = lax.all_to_all(outgoing, "seq", split_axis=0, concat_axis=0, tiled=True)
    fetched = incoming[my_slot]
    leading = jnp.stack([keys[: G * BLOCK], values[: G * BLOCK]])
    global_pairs = broadcast(leading, "seq", 0).reshape(2, G, BLOCK, features)
    extended = extended_2(jnp.stack([keys, values]), (("seq", 1),), BLOCK)
    left_pair = extended[:, :BLOCK]
    right_pair = extended[:, -BLOCK:]
    framed = jnp.concatenate([left_pair[:, None], own_pairs, right_pair[:, None]], axis=1)
    window = jnp.stack(
        [framed[:, 0:per_dev], framed[:, 1 : per_dev + 1], framed[:, 2 : per_dev + 2]], axis=2
    )
    global_slots = jnp.broadcast_to(global_pairs[:, None], (2, per_dev, G, BLOCK, features))
    randoms = fetched.reshape(per_dev, R, 2, BLOCK, features).transpose(2, 0, 1, 3, 4)
    gathered = jnp.concatenate([window, global_slots, randoms], axis=2)
    slot_keys = gathered[0].reshape(per_dev, slots_total, BLOCK, head_count, HD)
    slot_values = gathered[1].reshape(per_dev, slots_total, BLOCK, head_count, HD)
    block_index = device * per_dev + jnp.arange(per_dev)
    glob_index = jnp.arange(G)
    intersections = jnp.abs(glob_index[None, :] - block_index[:, None]) <= 1
    live_slots = jnp.concatenate(
        [
            (block_index >= 1)[:, None],
            jnp.ones((per_dev, 1), jnp.bool_),
            (block_index <= seq_count * per_dev - 2)[:, None],
            jnp.logical_not(intersections),
            jnp.ones((per_dev, R), jnp.bool_),
        ],
        axis=1,
    )
    query_blocks = queries.reshape(per_dev, BLOCK, head_count, HD)
    dout_blocks = out_grads.reshape(per_dev, BLOCK, head_count, HD)
    scores = (
        jnp.einsum("bxhd,bkyhd->bhxky", query_blocks, slot_keys, preferred_element_type=jnp.float32)
        * score_scale
    )
    scores = jnp.where(live_slots[:, None, None, :, None], scores, big_negative)
    row_max = jnp.max(scores, axis=(3, 4), keepdims=True)
    weights = jnp.exp(scores - row_max)
    row_total = jnp.sum(weights, axis=(3, 4), keepdims=True)
    probabilities = weights / row_total
    prob_low = probabilities.astype(jnp.bfloat16)
    prob_grads = jnp.einsum(
        "bxhd,bkyhd->bhxky", dout_blocks, slot_values, preferred_element_type=jnp.float32
    )
    row_dot = jnp.sum(probabilities * prob_grads, axis=(3, 4), keepdims=True)
    score_grads = (probabilities * (prob_grads - row_dot)).astype(jnp.bfloat16)
    query_grads = (
        jnp.einsum("bhxky,bkyhd->bxhd", score_grads, slot_keys, preferred_element_type=jnp.float32)
        * score_scale
    )
    key_terms = (
        jnp.einsum(
            "bhxky,bxhd->bkyhd", score_grads, query_blocks, preferred_element_type=jnp.float32
        )
        * score_scale
    )
    value_terms = jnp.einsum(
        "bhxky,bxhd->bkyhd", prob_low, dout_blocks, preferred_element_type=jnp.float32
    )
    pair_terms = jnp.stack([key_terms, value_terms]).reshape(
        2, per_dev, slots_total, BLOCK, features
    )
    framed_sum = jnp.pad(pair_terms[:, :, 0], ((0, 0), (0, 2), (0, 0), (0, 0)))
    framed_sum = framed_sum + jnp.pad(pair_terms[:, :, 1], ((0, 0), (1, 1), (0, 0), (0, 0)))
    framed_sum = framed_sum + jnp.pad(pair_terms[:, :, 2], ((0, 0), (2, 0), (0, 0), (0, 0)))
    totals = framed_sum[:, 1 : per_dev + 1]
    global_sum = jnp.sum(pair_terms[:, :, 3 : 3 + G], axis=1)
    rim_terms = jnp.concatenate([framed_sum[:, 0], framed_sum[:, -1]], axis=1)
    widened = extended_2(rim_terms.astype(jnp.bfloat16), (("seq", 1),), BLOCK).astype(
        rim_terms.dtype
    )
    totals = totals.at[:, 0].add(widened[:, :BLOCK])
    totals = totals.at[:, per_dev - 1].add(widened[:, -BLOCK:])
    target = jnp.where(my_usable, my_slot, seq_count * capacity)
    rand_terms = (
        pair_terms[:, :, 3 + G :].reshape(2, rand_count, BLOCK, features).transpose(1, 0, 2, 3)
    )
    outgoing_back = (
        jnp.zeros((seq_count * capacity, 2, BLOCK, features), jnp.float32)
        .at[target]
        .set(rand_terms, mode="drop")
    )
    arrived = lax.all_to_all(
        outgoing_back.astype(jnp.bfloat16), "seq", split_axis=0, concat_axis=0, tiled=True
    ).astype(outgoing_back.dtype)
    collected = jnp.einsum(
        "dcb,dcsxf->sbxf",
        chooser,
        arrived.reshape(seq_count, capacity, 2, BLOCK, features),
        precision=lax.Precision.HIGHEST,
    )
    everywhere = lax.psum(global_sum, "seq")
    padded_global = jnp.pad(everywhere, ((0, 0), (0, per_dev - G), (0, 0), (0, 0))) * (
        device == 0
    ).astype(jnp.float32)
    totals = totals + collected + padded_global
    grad_rows = query_grads.reshape(tokens, features).astype(jnp.bfloat16)
    key_rows = totals[0].reshape(tokens, features).astype(jnp.bfloat16)
    value_rows = totals[1].reshape(tokens, features).astype(jnp.bfloat16)
    return (
        lax.all_to_all(grad_rows, "head", split_axis=0, concat_axis=1, tiled=True),
        lax.all_to_all(key_rows, "head", split_axis=0, concat_axis=1, tiled=True),
        lax.all_to_all(value_rows, "head", split_axis=0, concat_axis=1, tiled=True),
    )


def solution(mesh):
    in_specs = (
        P(("seq", "head"), None),
        P(("seq", "head"), None),
        P(("seq", "head"), None),
        P(("seq", "head"), None),
        P(),
    )
    out_specs = (P(("seq", "head"), None), P(("seq", "head"), None), P(("seq", "head"), None))
    return jax.shard_map(
        on_device, mesh=mesh, in_specs=in_specs, out_specs=out_specs, check_vma=False
    )
```

profile of v0, /device:TPU:12, one launch (start us, length us, event | category | flops | bytes accessed | tf_op | source)
XLA Modules:
  0.0 629.3 jit_solution(11940915800313136939)
XLA Ops:
  7.2 2.1 copy.326
  9.3 3.5 all-to-all-start.3
  12.8 2.0 copy.328
  16.3 6.7 %all-to-all-done.3 = bf16[160,4,512]{2,0,1:T(8,128)(2,1)S(1)} async-done(((bf16[160,4,512]{2,0,1:T(8,128)(2,1)}), bf16[160,4,512]{2,0,1:T(8,128)(2,1)S(1)}, u32[]{:S(2)}, u32[]{:S(2)}) %all-to-all-start.3) | async-done | bytes 655392 | tf_op jit(solution)/shard_map/all_to_all | solution.py:46
  23.0 3.5 all-to-all-start
  28.1 8.6 %all-to-all-done = bf16[160,4,512]{2,0,1:T(8,128)(2,1)S(1)} async-done(((bf16[160,4,512]{2,0,1:T(8,128)(2,1)}), bf16[160,4,512]{2,0,1:T(8,128)(2,1)S(1)}, u32[]{:S(2)}, u32[]{:S(2)}) %all-to-all-start) | async-done | bytes 655392 | tf_op jit(solution)/shard_map/all_to_all | solution.py:47
  36.7 3.5 all-to-all-start.1
  41.8 8.6 %all-to-all-done.1 = bf16[160,4,512]{2,0,1:T(8,128)(2,1)S(1)} async-done(((bf16[160,4,512]{2,0,1:T(8,128)(2,1)}), bf16[160,4,512]{2,0,1:T(8,128)(2,1)S(1)}, u32[]{:S(2)}, u32[]{:S(2)}) %all-to-all-start.1) | async-done | bytes 655392 | tf_op jit(solution)/shard_map/all_to_all | solution.py:48
  50.4 4.2 all-to-all-start.4
  56.5 4.1 copy.220
  60.6 4.3 all-to-all-done.4
  64.9 6.2 all-to-all-start.2
  72.3 2.5 collective-permute-start.1
  74.8 4.5 collective-permute-start
  79.9 2.3 reshape.357
  82.2 1.6 maximum_select_fusion
  83.9 2.3 reshape.358
  86.2 106.0 %collective-permute-done.1 = bf16[2,64,512]{2,1,0:T(8,128)(2,1)} collective-permute-done((bf16[2,64,512]{2,1,0:T(8,128)(2,1)}, bf16[2,64,512]{2,1,0:T(8,128)(2,1)}, u32[]{:S(2)}, u32[]{:S(2)}) %collective-permute-start.1) | collective-permute-done | bytes 131104 | tf_op jit(solution)/shard_map/ppermute | solution.py:28
  194.5 2.1 fusion.23
  196.6 1.8 copy_dynamic-update-slice_fusion.1
  199.6 1.8 copy_dynamic-update-slice_fusion
  201.4 24.9 %all-reduce.7.cloned.1.call-done = bf16[2,2,64,512]{3,2,1,0:T(8,128)(2,1)} async-done(((bf16[2,2,64,512]{3,2,1,0:T(8,128)(2,1)}), bf16[2,2,64,512]{3,2,1,0:T(8,128)(2,1)}) %all-reduce.7.cloned.1.call-update) | async-done | bytes 262160 | tf_op jit(solution)/shard_map/psum | solution.py:17
  226.3 2.8 broadcast_dynamic-update-slice_fusion
  229.1 5.2 gather_fusion.1
  234.2 4.5 bitcast_dynamic-update-slice_fusion
  238.7 9.6 %fusion.59 = (bf16[1,10,8,64,512]{4,3,2,1,0:T(8,128)(2,1)}, bf16[1,10,8,64,512]{4,3,2,1,0:T(8,128)(2,1)}) fusion(bf16[2,10,8,64,512]{4,3,2,1,0:T(8,128)(2,1)} %bitcast_dynamic-update-slice_fusion), kind=kLoop, calls=%fused_computation.112 | loop fusion | bytes 20971520 | tf_op jit(solution)/shard_map/slice | solution.py:98
  248.3 8.3 %reshape_squeeze.8 = bf16[10,8,64,4,128]{4,3,2,1,0:T(4,128)(2,1)} reshape(bf16[1,10,8,64,512]{4,3,2,1,0:T(8,128)(2,1)} %get-tuple-element.37) | data formatting | bytes 10485760 | tf_op jit(solution)/shard_map/reshape;squeeze | solution.py:98
  256.6 8.4 %reshape_squeeze.9 = bf16[10,8,64,4,128]{4,3,2,1,0:T(4,128)(2,1)} reshape(bf16[1,10,8,64,512]{4,3,2,1,0:T(8,128)(2,1)} %get-tuple-element.38) | data formatting | bytes 10485760 | tf_op jit(solution)/shard_map/reshape;squeeze | solution.py:99
  265.0 4.2 bitcast_reduce_fusion
  269.2 3.1 fusion.5
  272.3 5.8 fusion.18
  278.1 6.3 fusion
  284.4 6.8 %fusion.2 = bf16[10,4,64,8,64]{2,4,3,1,0:T(8,128)(2,1)S(1)} fusion(f32[10,4,8,64,64]{4,3,2,1,0:T(8,128)} %get-tuple-element.50, f32[10,4,64]{2,1,0:T(4,128)S(1)} %get-tuple-element.49, f32[10,4,64]{2,1,0:T(4,128)S(1)} %fusion.5, f32[10,4,64]{2,1,0:T(4,128)S(1)} %get-tuple-element.47, f32[10,4,8,64,64]{4,3,2,1,0:T(8,128)S(1)} %get-tuple-element.48, ...), kind=kLoop, calls=%fused_computation.7 | loop fusion | flops 9175040 | bytes 13138000 | tf_op jit(solution)/shard_map/convert_element_type | solution.py:129
  291.2 2.2 copy-done
  293.4 4.7 multiply_bitcast_fusion
  298.1 18.2 %copy.267 = f32[10,8,64,4,128]{4,3,2,0,1:T(4,128)} copy(f32[10,8,64,4,128]{4,2,1,3,0:T(8,128)} %multiply_bitcast_fusion) | data formatting | bytes 20971520 | tf_op jit(solution)/shard_map/stack | solution.py:143
  316.3 12.9 %reshape.405 = f32[1,10,8,64,512]{4,3,0,1,2:T(8,128)} reshape(f32[10,8,64,4,128]{4,3,2,0,1:T(4,128)} %copy.267) | data formatting | bytes 20971520 | tf_op jit(solution)/shard_map/stack | solution.py:143
  329.1 10.2 %constant_dynamic-update-slice_fusion.1 = f32[2,10,8,64,512]{4,3,0,1,2:T(8,128)} fusion(f32[1,10,8,64,512]{4,3,0,1,2:T(8,128)} %reshape.405), kind=kLoop, calls=%fused_computation.82 | loop fusion | bytes 20971520
  339.4 18.0 %copy.270 = f32[10,8,64,4,128]{4,3,2,0,1:T(4,128)} copy(f32[10,8,64,4,128]{4,2,1,3,0:T(8,128)} %fusion.18) | data formatting | bytes 20971520 | tf_op jit(solution)/shard_map/stack | solution.py:143
  357.4 12.9 %reshape.406 = f32[1,10,8,64,512]{4,3,0,1,2:T(8,128)} reshape(f32[10,8,64,4,128]{4,3,2,0,1:T(4,128)} %copy.270) | data formatting | bytes 20971520 | tf_op jit(solution)/shard_map/stack | solution.py:143
  370.3 10.1 %constant_dynamic-update-slice_fusion = f32[2,10,8,64,512]{4,3,0,1,2:T(8,128)} fusion(f32[2,10,8,64,512]{4,3,0,1,2:T(8,128)} %constant_dynamic-update-slice_fusion.1, f32[1,10,8,64,512]{4,3,0,1,2:T(8,128)} %reshape.406), kind=kLoop, calls=%fused_computation.81 | loop fusion | bytes 20971520 | tf_op jit(solution)/shard_map/stack | solution.py:143
  380.4 4.3 slice.161
  386.3 4.2 copy.244
  390.5 5.3 broadcast_in_dim.28
  395.8 15.2 %scatter_fusion = f32[40,2,64,512]{3,2,1,0:T(8,128)} fusion(f32[40,2,64,512]{3,2,1,0:T(8,128)} %broadcast_in_dim.28, s32[30]{0:T(128)S(1)} %fusion.56, f32[30,2,64,512]{3,2,1,0:T(8,128)} %copy.244), kind=kCustom, calls=%fused_computation.2 | custom fusion | bytes 23593080 | tf_op jit(solution)/shard_map/scatter | solution.py:164
  411.0 7.1 %convert_element_type.71 = bf16[40,2,64,512]{3,2,1,0:T(8,128)(2,1)} convert(f32[40,2,64,512]{3,2,1,0:T(8,128)} %scatter_fusion) | non-fusion elementwise | flops 2621440 | bytes 15728640 | tf_op jit(solution)/shard_map/convert_element_type | solution.py:167
  418.1 5.5 all-to-all-start.6
  423.6 4.5 slice_bitcast_fusion.2
  428.1 2.7 fusion.58
  430.9 2.5 collective-permute-start.3
  433.4 4.5 collective-permute-start.2
  437.9 4.5 fusion.36
  442.4 3.1 slice_reduce_fusion
  447.2 2.1 slice.156
  450.5 96.0 %collective-permute-done.3 = bf16[2,64,512]{2,1,0:T(8,128)(2,1)S(1)} collective-permute-done((bf16[2,64,512]{2,1,0:T(8,128)(2,1)S(1)}, bf16[2,64,512]{2,1,0:T(8,128)(2,1)S(1)}, u32[]{:S(2)}, u32[]{:S(2)}) %collective-permute-start.3) | collective-permute-done | bytes 131104 | tf_op jit(solution)/shard_map/ppermute | solution.py:28
  547.5 3.7 copy.242
  551.6 6.4 %scatter-add.9 = f32[2,10,64,512]{3,1,2,0:T(8,128)} dynamic-update-slice(f32[2,10,64,512]{3,1,2,0:T(8,128)} %copy.242, f32[2,1,64,512]{3,1,2,0:T(1,128)S(1)} %copy_add_fusion, s32[]{:T(128)} %constant.107.clone.1, s32[]{:T(128)} %constant.123.clone.1, s32[]{:T(128)} %constant.107.clone.1, s32[]{:T(128)} %constant.107.clone.1) | dynamic-update-slice | bytes 524292 | tf_op jit(solution)/shard_map/scatter-add | solution.py:156
  558.0 3.5 all-to-all-start.5
  561.5 22.1 %all-reduce.9.cloned.1.call-done = f32[2,2,64,512]{3,1,2,0:T(2,128)} async-done(((f32[2,2,64,512]{3,1,2,0:T(2,128)}), f32[2,2,64,512]{3,1,2,0:T(2,128)}) %all-reduce.9.cloned.1.call-update) | async-done | bytes 524304 | tf_op jit(solution)/shard_map/psum | solution.py:175
  583.6 8.7 %fusion.17 = bf16[2,10,64,512]{3,1,2,0:T(8,128)(2,1)S(1)} fusion(f32[2,10,64,512]{3,1,2,0:T(8,128)} %scatter-add.9, f32[2,2,64,512]{3,1,2,0:T(2,128)} %all-reduce.9.cloned.1.call-done, bf16[8,5,2,64,512]{4,3,2,1,0:T(8,128)(2,1)} %bitcast.53, f32[]{:T(128)S(6)} %convert_element_type.72, f32[8,5,10]{0,2,1:T(8,128)S(1)} %copy-done.7), kind=kOutput, calls=%fused_computation.28 | convolution fusion | flops 317194240 | bytes 9700932 | tf_op jit(solution)/shard_map/dcb,dcsxf->sbxf/dot_general | solution.py:169
  593.7 3.5 all-to-all-start.7
  598.3 9.0 %all-to-all-done.7 = bf16[4,160,512]{2,1,0:T(8,128)(2,1)S(1)} async-done(((bf16[4,160,512]{2,1,0:T(8,128)(2,1)}), bf16[4,160,512]{2,1,0:T(8,128)(2,1)S(1)}, u32[]{:S(2)}, u32[]{:S(2)}) %all-to-all-start.7) | async-done | bytes 655392 | tf_op jit(solution)/shard_map/all_to_all | solution.py:185
  607.4 3.5 all-to-all-start.8
  612.7 8.4 %all-to-all-done.8 = bf16[4,160,512]{2,1,0:T(8,128)(2,1)S(1)} async-done(((bf16[4,160,512]{2,1,0:T(8,128)(2,1)}), bf16[4,160,512]{2,1,0:T(8,128)(2,1)S(1)}, u32[]{:S(2)}, u32[]{:S(2)}) %all-to-all-start.8) | async-done | bytes 655392 | tf_op jit(solution)/shard_map/all_to_all | solution.py:186
  (85 shorter events, 23.0 us)
Async XLA Ops:
  7.2 20.0 %copy-start.3 = (bf16[160,2048]{1,0:T(8,128)(2,1)S(1)}, bf16[160,2048]{1,0:T(8,128)(2,1)}, u32[]{:S(2)}) copy-start(bf16[160,2048]{1,0:T(8,128)(2,1)} %param.11) | copy-start | bytes 1966084
  7.2 33.3 %copy-start.4 = (bf16[160,2048]{1,0:T(8,128)(2,1)S(1)}, bf16[160,2048]{1,0:T(8,128)(2,1)}, u32[]{:S(2)}) copy-start(bf16[160,2048]{1,0:T(8,128)(2,1)} %param.12) | copy-start | bytes 1966084
  9.3 13.7 %all-to-all-start.3 = ((bf16[160,4,512]{2,0,1:T(8,128)(2,1)}), bf16[160,4,512]{2,0,1:T(8,128)(2,1)S(1)}, u32[]{:S(2)}, u32[]{:S(2)}) async-start(bf16[160,4,512]{2,0,1:T(8,128)(2,1)} %bitcast.179), calls=%async_computation.3 | async-start | bytes 1310720 | tf_op jit(solution)/shard_map/all_to_all | solution.py:46
  23.0 18.4 %copy-start.2 = (bf16[160,4,512]{2,0,1:T(8,128)(2,1)}, bf16[160,4,512]{2,0,1:T(8,128)(2,1)S(1)}, u32[]{:S(2)}) copy-start(bf16[160,4,512]{2,0,1:T(8,128)(2,1)S(1)} %all-to-all-done.3) | copy-start | bytes 1966084
  23.0 13.7 %all-to-all-start = ((bf16[160,4,512]{2,0,1:T(8,128)(2,1)}), bf16[160,4,512]{2,0,1:T(8,128)(2,1)S(1)}, u32[]{:S(2)}, u32[]{:S(2)}) async-start(bf16[160,4,512]{2,0,1:T(8,128)(2,1)} %bitcast.181), calls=%async_computation | async-start | bytes 1310720 | tf_op jit(solution)/shard_map/all_to_all | solution.py:47
  36.7 13.7 %all-to-all-start.1 = ((bf16[160,4,512]{2,0,1:T(8,128)(2,1)}), bf16[160,4,512]{2,0,1:T(8,128)(2,1)S(1)}, u32[]{:S(2)}, u32[]{:S(2)}) async-start(bf16[160,4,512]{2,0,1:T(8,128)(2,1)} %bitcast.180), calls=%async_computation.1 | async-start | bytes 1310720 | tf_op jit(solution)/shard_map/all_to_all | solution.py:48
  40.3 1.0 copy-start.6
  50.4 14.5 %all-to-all-start.4 = ((bf16[160,4,512]{2,0,1:T(8,128)(2,1)}), bf16[160,4,512]{2,0,1:T(8,128)(2,1)}, u32[]{:S(2)}, u32[]{:S(2)}) async-start(bf16[160,4,512]{2,0,1:T(8,128)(2,1)} %bitcast.202), calls=%async_computation.4 | async-start | bytes 1310720 | tf_op jit(solution)/shard_map/all_to_all | solution.py:49
  64.9 164.2 %all-to-all-start.2 = ((bf16[40,2,64,512]{3,2,1,0:T(8,128)(2,1)}), bf16[40,2,64,512]{3,2,1,0:T(8,128)(2,1)}, u32[]{:S(2)}, u32[]{:S(2)}) async-start(bf16[40,2,64,512]{3,2,1,0:T(8,128)(2,1)} %bitcast.185), calls=%async_computation.2 | async-start | bytes 10485760 | tf_op jit(solution)/shard_map/all_to_all | solution.py:84
  71.1 155.2 %all-reduce.7.cloned.1.call-start = ((), (), s32[]{:S(2)}) async-start(), calls=%async_computation.9 | async-start | bytes 524288 | tf_op jit(solution)/shard_map/psum | solution.py:17
  72.3 119.9 %collective-permute-start.1 = (bf16[2,64,512]{2,1,0:T(8,128)(2,1)}, bf16[2,64,512]{2,1,0:T(8,128)(2,1)}, u32[]{:S(2)}, u32[]{:S(2)}) collective-permute-start(bf16[2,64,512]{2,1,0:T(8,128)(2,1)} %get-tuple-element.45), channel_id=1, source_target_pairs={{4,0},{8,4},{12,8},{16,12},{20,16},{24,20},{28,24},{5,1},{9,5},{13... | collective-permute-start | bytes 393224 | tf_op jit(solution)/shard_map/ppermute | solution.py:28
  74.8 118.6 %collective-permute-start = (bf16[2,64,512]{2,1,0:T(8,128)(2,1)}, bf16[2,64,512]{2,1,0:T(8,128)(2,1)}, u32[]{:S(2)}, u32[]{:S(2)}) collective-permute-start(bf16[2,64,512]{2,1,0:T(8,128)(2,1)} %get-tuple-element.46), channel_id=1, source_target_pairs={{0,4},{4,8},{8,12},{12,16},{16,20},{20,24},{24,28},{1,5},{5,9},{9,... | collective-permute-start | bytes 393224 | tf_op jit(solution)/shard_map/ppermute | solution.py:27
  256.6 8.4 %copy-start.1 = (bf16[10,64,4,128]{3,2,1,0:T(4,128)(2,1)S(1)}, bf16[10,64,4,128]{3,2,1,0:T(4,128)(2,1)}, u32[]{:S(2)}) copy-start(bf16[10,64,4,128]{3,2,1,0:T(4,128)(2,1)} %reshape.357) | copy-start | bytes 1966084
  269.2 3.1 copy-start.5
  269.2 8.9 %slice-start.2 = ((s8[5242880]{0:T(1024)(128)(4,1)}), s8[4194304]{0:T(1024)(128)(4,1)S(1)}, s32[]{:S(2)}) async-start(s8[5242880]{0:T(1024)(128)(4,1)} %bitcast.195), calls=%async_computation.13 | async-start | bytes 8388608
  272.3 5.8 slice-start.3
  291.2 2.2 copy-start
  418.1 19.8 %slice-start = ((s8[5242880]{0:T(1024)(128)(4,1)}), s8[1048576]{0:T(1024)(128)(4,1)S(1)}, s32[]{:S(2)}) async-start(s8[5242880]{0:T(1024)(128)(4,1)} %bitcast.182), calls=%async_computation.11 | async-start | bytes 2097152
  418.1 139.9 %all-to-all-start.6 = ((bf16[40,2,64,512]{3,2,1,0:T(8,128)(2,1)}), bf16[40,2,64,512]{3,2,1,0:T(8,128)(2,1)}, u32[]{:S(2)}, u32[]{:S(2)}) async-start(bf16[40,2,64,512]{3,2,1,0:T(8,128)(2,1)} %convert_element_type.71), calls=%async_computation.6 | async-start | bytes 10485760 | tf_op jit(solution)/shard_map/all_to_all | solution.py:166
  423.6 160.0 %all-reduce.9.cloned.1.call-start = ((), (), s32[]{:S(2)}) async-start(), calls=%async_computation.10 | async-start | bytes 1048576 | tf_op jit(solution)/shard_map/psum | solution.py:175
  423.6 14.3 %slice-start.1 = ((s8[5242880]{0:T(1024)(128)(4,1)}), s8[4194304]{0:T(1024)(128)(4,1)S(1)}, s32[]{:S(2)}) async-start(s8[5242880]{0:T(1024)(128)(4,1)} %bitcast.182), calls=%async_computation.12 | async-start | bytes 8388608
  430.9 115.6 %collective-permute-start.3 = (bf16[2,64,512]{2,1,0:T(8,128)(2,1)S(1)}, bf16[2,64,512]{2,1,0:T(8,128)(2,1)S(1)}, u32[]{:S(2)}, u32[]{:S(2)}) collective-permute-start(bf16[2,64,512]{2,1,0:T(8,128)(2,1)S(1)} %get-tuple-element.44), channel_id=1, source_target_pairs={{4,0},{8,4},{12,8},{16,12},{20,16},{24,20},{28,24},{5,1},{9,5},{13... | collective-permute-start | bytes 393224 | tf_op jit(solution)/shard_map/ppermute | solution.py:28
  433.4 113.1 %collective-permute-start.2 = (bf16[2,64,512]{2,1,0:T(8,128)(2,1)S(1)}, bf16[2,64,512]{2,1,0:T(8,128)(2,1)}, u32[]{:S(2)}, u32[]{:S(2)}) collective-permute-start(bf16[2,64,512]{2,1,0:T(8,128)(2,1)S(1)} %get-tuple-element.43), channel_id=1, source_target_pairs={{0,4},{4,8},{8,12},{12,16},{16,20},{20,24},{24,28},{1,5},{5,9},{9,... | collective-permute-start | bytes 393224 | tf_op jit(solution)/shard_map/ppermute | solution.py:27
  547.5 36.1 %copy-start.7 = (f32[8,5,10]{0,2,1:T(8,128)S(1)}, f32[8,5,10]{0,2,1:T(8,128)}, u32[]{:S(2)}) copy-start(f32[8,5,10]{0,2,1:T(8,128)} %copy-done.6) | copy-start | bytes 4804
  558.0 35.7 %all-to-all-start.5 = ((bf16[4,160,512]{2,1,0:T(8,128)(2,1)}), bf16[4,160,512]{2,1,0:T(8,128)(2,1)S(1)}, u32[]{:S(2)}, u32[]{:S(2)}) async-start(bf16[4,160,512]{2,1,0:T(8,128)(2,1)} %convert_element_type.68), calls=%async_computation.5 | async-start | bytes 1310720 | tf_op jit(solution)/shard_map/all_to_all | solution.py:184
  593.7 13.7 %all-to-all-start.7 = ((bf16[4,160,512]{2,1,0:T(8,128)(2,1)}), bf16[4,160,512]{2,1,0:T(8,128)(2,1)S(1)}, u32[]{:S(2)}, u32[]{:S(2)}) async-start(bf16[4,160,512]{2,1,0:T(8,128)(2,1)} %bitcast.58), calls=%async_computation.7 | async-start | bytes 1310720 | tf_op jit(solution)/shard_map/all_to_all | solution.py:185
  607.4 13.7 %all-to-all-start.8 = ((bf16[4,160,512]{2,1,0:T(8,128)(2,1)}), bf16[4,160,512]{2,1,0:T(8,128)(2,1)S(1)}, u32[]{:S(2)}, u32[]{:S(2)}) async-start(bf16[4,160,512]{2,1,0:T(8,128)(2,1)} %bitcast.60), calls=%async_computation.8 | async-start | bytes 1310720 | tf_op jit(solution)/shard_map/all_to_all | solution.py:186
Sparse Core Ops, SparseCore 0:
  84.0 142.1 all-reduce.6
  450.6 132.9 all-reduce.8
where the time goes:
time: 639 us; the launch traced here: 629 us
  waiting for transfers between devices  295 us (46%)
  local copies, waits for them, and re-layouts  202 us (32%)
  starting transfers between devices  50.8 us (8%)
  matrix products  35.6 us (6%)
  other arithmetic  31.1 us (5%)
  between operations  14.9 us (2%)
    ppermute x2, waiting for transfers between devices, extended_2(): after = lax.ppermute(leading, axis, down)  202 us
    another operation x5, local copies, waits for them, and re-layouts, on_device(): jnp.stack([key_terms, value_terms])  72.1 us
    psum x1, waiting for transfers between devices, broadcast(): return lax.psum(block, axis)  24.9 us
    psum x1, waiting for transfers between devices, on_device(): everywhere = lax.psum(global_sum, 'seq')  22.1 us
    unnamed x30, local copies, waits for them, and re-layouts  20.1 us
    scatter x1, local copies, waits for them, and re-layouts, on_device(): outgoing_back = jnp.zeros((seq_count * capacity, 2, BLOCK, features), jnp...  15.2 us
  transfers between devices with their start and end apart: 15, of which 10 were waited for; matrix products, arithmetic and copies ran while one was open for 12% of the time, Pallas kernels for 0%

commit v1 on v0

--- a/solution.py
+++ b/solution.py
@@ -1,6 +1,10 @@
+import functools
+
 import jax
 import jax.numpy as jnp
 from jax import lax
+from jax.experimental import pallas as pl
+from jax.experimental.pallas import tpu as pltpu
 from jax.sharding import PartitionSpec as P
 
 HD = 128
@@ -82,7 +86,10 @@
     ).astype(jnp.bfloat16)
     outgoing = served.reshape(seq_count * capacity, 2, BLOCK, features)
     incoming = lax.all_to_all(outgoing, "seq", split_axis=0, concat_axis=0, tiled=True)
-    fetched = incoming[my_slot]
+    wanted = (my_slot[:, None] == jnp.arange(seq_count * capacity)[None, :]).astype(jnp.bfloat16)
+    fetched = jnp.einsum(
+        "ro,osxf->rsxf", wanted, incoming, preferred_element_type=jnp.float32
+    ).astype(jnp.bfloat16)
     leading = jnp.stack([keys[: G * BLOCK], values[: G * BLOCK]])
     global_pairs = broadcast(leading, "seq", 0).reshape(2, G, BLOCK, features)
     extended = extended_2(jnp.stack([keys, values]), (("seq", 1),), BLOCK)
@@ -187,15 +194,234 @@
     )
 
 
+LOG2E = 1.4426950408889634
+
+
+def attend_units(units, block_count, rand_of, q_of, do_of, kf, vf, dkf, dvf, put_dq):
+    slots_total = 3 + G + R
+    f32, bf16 = jnp.float32, jnp.bfloat16
+    lanes = sum(rows for _, rows, _ in units)
+    lane = lax.broadcasted_iota(jnp.int32, (1, lanes), 1)
+    slot_ids, biases = [], []
+    for _, _, j in units:
+        slot_ids.append(
+            [jnp.maximum(j - 1, 0), j, jnp.minimum(j + 1, block_count - 1)]
+            + list(range(G))
+            + [rand_of(j, r) for r in range(R)]
+        )
+        live = {0: j >= 1, 2: j <= block_count - 2}
+        for i in range(G):
+            live[3 + i] = jnp.abs(i - j) > 1
+        biases.append({s: jnp.where(ok, 0.0, big_negative).astype(f32) for s, ok in live.items()})
+
+    def slot_rows(ref, b):
+        if isinstance(b, int):
+            return ref[b * BLOCK : (b + 1) * BLOCK, :]
+        return ref[pl.ds(pl.multiple_of(b * BLOCK, BLOCK), BLOCK), :]
+
+    def side_by_side(ref):
+        return jnp.concatenate(
+            [jnp.concatenate([slot_rows(ref, b) for b in ids], axis=0) for ids in slot_ids], axis=1
+        )
+
+    def diagonal(get):
+        strips = []
+        for at, (first, rows, _) in enumerate(units):
+            blank = jnp.zeros((rows, HD), bf16)
+            strips.append(
+                jnp.concatenate(
+                    [get(first, rows) if i == at else blank for i in range(len(units))], axis=1
+                )
+            )
+        return jnp.concatenate(strips, axis=0)
+
+    k_all, v_all = side_by_side(kf), side_by_side(vf)
+    q_diag, do_diag = diagonal(q_of), diagonal(do_of)
+    across = (((1,), (1,)), ((), ()))
+    raw = lax.dot_general(k_all, q_diag, across, preferred_element_type=f32)
+    factor = HD ** (-0.5) * LOG2E
+    parts = []
+    for s in range(slots_total):
+        part = raw[s * BLOCK : (s + 1) * BLOCK] * factor
+        if s in biases[0]:
+            bias = jnp.full((1, lanes), 0.0, f32) + biases[0][s]
+            start = 0
+            for at in range(1, len(units)):
+                start += units[at - 1][1]
+                bias = jnp.where(lane >= start, biases[at][s], bias)
+            part = part + bias
+        parts.append(part)
+    scores = jnp.concatenate(parts, axis=0)
+    weights = jnp.exp2(scores - jnp.max(scores, axis=0, keepdims=True))
+    probs = weights * (1.0 / jnp.sum(weights, axis=0, keepdims=True))
+    prob_grads = lax.dot_general(v_all, do_diag, across, preferred_element_type=f32)
+    row_dot = jnp.sum(probs * prob_grads, axis=0, keepdims=True)
+    score_grads = (probs * (prob_grads - row_dot)).astype(bf16)
+    dv = jnp.dot(probs.astype(bf16), do_diag, preferred_element_type=f32)
+    dk = jnp.dot(score_grads, q_diag, preferred_element_type=f32)
+    dq = lax.dot_general(
+        score_grads, k_all, (((0,), (0,)), ((), ())), preferred_element_type=f32
+    ) * (HD ** (-0.5))
+    for at, ids in enumerate(slot_ids):
+        cols = slice(at * HD, (at + 1) * HD)
+        for s, b in enumerate(ids):
+            rows = slice(s * BLOCK, (s + 1) * BLOCK)
+            if isinstance(b, int):
+                where = pl.ds(b * BLOCK, BLOCK)
+            else:
+                where = pl.ds(pl.multiple_of(b * BLOCK, BLOCK), BLOCK)
+            dkf[where, :] += dk[rows, cols]
+            dvf[where, :] += dv[rows, cols]
+    start = 0
+    for at, (first, rows, _) in enumerate(units):
+        put_dq(first, rows, dq[start : start + rows, at * HD : (at + 1) * HD].astype(bf16))
+        start += rows
+
+
+def attend_kernel(chunks, core_ref, rand_ref, qd_ref, own_ref, sib_ref, dq_ref, down_ref, dsib_ref,
+                  kf, vf, dkf, dvf):
+    span = qd_ref.shape[2]
+    half = BLOCK // 2
+    per_pair = 2 * span // BLOCK
+    block_count = chunks * per_pair
+    core = core_ref[0]
+
+    def rows_at(g, which):
+        return pl.ds(pl.multiple_of(g * 2 * span + which * span, half), span)
+
+    def lay(g, carry):
+        mine, other = rows_at(g, core), rows_at(g, 1 - core)
+        kf[mine, :] = own_ref[g, 0]
+        vf[mine, :] = own_ref[g, 1]
+        kf[other, :] = sib_ref[g, 0]
+        vf[other, :] = sib_ref[g, 1]
+        zeros = jnp.zeros((span, HD), jnp.float32)
+        for ref in (dkf, dvf):
+            ref[mine, :] = zeros
+            ref[other, :] = zeros
+        return carry
+
+    lax.fori_loop(0, chunks, lay, 0)
+
+    def run(units):
+        attend_units(
+            [(first, rows, j) for first, rows, j in units],
+            block_count,
+            lambda j, r: rand_ref[j * R + r],
+            lambda at, rows: qd_ref[at[0], 0, pl.ds(pl.multiple_of(at[1], half), rows), :],
+            lambda at, rows: qd_ref[at[0], 1, pl.ds(pl.multiple_of(at[1], half), rows), :],
+            kf, vf, dkf, dvf,
+            put,
+        )
+
+    def put(at, rows, values):
+        dq_ref[at[0], pl.ds(pl.multiple_of(at[1], half), rows), :] = values
+
+    def whole_blocks(g, carry):
+        run(
+            [
+                ((g, core * half + i * BLOCK), BLOCK, g * per_pair + core * 3 + i)
+                for i in range(2)
+            ]
+        )
+        return carry
+
+    lax.fori_loop(0, chunks, whole_blocks, 0)
+
+    def half_blocks(t, carry):
+        run(
+            [
+                ((t * 4 + i, (1 - core) * 2 * BLOCK), half, (t * 4 + i) * per_pair + 2)
+                for i in range(4)
+            ]
+        )
+        return carry
+
+    lax.fori_loop(0, chunks // 4, half_blocks, 0)
+
+    def hand_over(g, carry):
+        mine, other = rows_at(g, core), rows_at(g, 1 - core)
+        scale = HD ** (-0.5)
+        down_ref[g, 0] = dkf[mine, :] * scale
+        down_ref[g, 1] = dvf[mine, :]
+        dsib_ref[g, 0] = (dkf[other, :] * scale).astype(jnp.bfloat16)
+        dsib_ref[g, 1] = dvf[other, :].astype(jnp.bfloat16)
+        return carry
+
+    lax.fori_loop(0, chunks, hand_over, 0)
+
+
+def on_chip_pair(seq_count, head_devices, query, key, value, grad_out, rand_blocks):
+    both = ("seq", "head")
+    count = seq_count * head_devices
+    chunks = count // 2
+    groups = [[i for i in range(count) if i % 2 == core] for core in range(2)]
+    swap = [(i, i ^ 1) for i in range(head_devices)]
+    span = query.shape[0]
+    core = lax.rem(lax.axis_index("head"), 2)
+
+    def spread(*arrays):
+        cut = jnp.stack([a.reshape(span, chunks, HD).transpose(1, 0, 2) for a in arrays], axis=1)
+        return lax.all_to_all(
+            cut, both, split_axis=0, concat_axis=0, axis_index_groups=groups, tiled=True
+        )
+
+    own = spread(key, value)
+    rows = spread(query, grad_out)
+    sib = lax.ppermute(own, "head", swap)
+    vmem = pl.BlockSpec(memory_space=pltpu.VMEM)
+    smem = pl.BlockSpec(memory_space=pltpu.SMEM)
+    total = chunks * 2 * span
+    dq, down, dsib = pl.pallas_call(
+        functools.partial(attend_kernel, chunks),
+        out_shape=(
+            jax.ShapeDtypeStruct((chunks, span, HD), jnp.bfloat16),
+            jax.ShapeDtypeStruct((chunks, 2, span, HD), jnp.float32),
+            jax.ShapeDtypeStruct((chunks, 2, span, HD), jnp.bfloat16),
+        ),
+        in_specs=[smem, smem, vmem, vmem, vmem],
+        out_specs=(vmem, vmem, vmem),
+        scratch_shapes=[
+            pltpu.VMEM((total, HD), jnp.bfloat16),
+            pltpu.VMEM((total, HD), jnp.bfloat16),
+            pltpu.VMEM((total, HD), jnp.float32),
+            pltpu.VMEM((total, HD), jnp.float32),
+        ],
+        compiler_params=pltpu.CompilerParams(vmem_limit_bytes=40 * 2**20),
+    )(core.reshape(1), rand_blocks.reshape(-1), rows, own, sib)
+    part = lax.ppermute(dsib, "head", swap)
+    summed = (down + part.astype(jnp.float32)).astype(jnp.bfloat16)
+
+    def collect(cut):
+        return lax.all_to_all(
+            cut, both, split_axis=0, concat_axis=0, axis_index_groups=groups, tiled=True
+        )
+
+    def flat(cut):
+        return cut.transpose(1, 0, 2).reshape(span, chunks * HD)
+
+    dq = flat(collect(dq))
+    both_grads = collect(summed)
+    return dq, flat(both_grads[:, 0]), flat(both_grads[:, 1])
+
+
 def solution(mesh):
-    in_specs = (
-        P(("seq", "head"), None),
-        P(("seq", "head"), None),
-        P(("seq", "head"), None),
-        P(("seq", "head"), None),
-        P(),
-    )
-    out_specs = (P(("seq", "head"), None), P(("seq", "head"), None), P(("seq", "head"), None))
-    return jax.shard_map(
-        on_device, mesh=mesh, in_specs=in_specs, out_specs=out_specs, check_vma=False
-    )
+    rows = P(("seq", "head"), None)
+    seq_count, head_devices = mesh.shape["seq"], mesh.shape["head"]
+
+    def run(query, key, value, grad_out, rand_blocks):
+        count = seq_count * head_devices
+        heads = query.shape[1] // HD
+        span = query.shape[0] // count
+        body = on_device
+        if head_devices % 2 == 0 and count == 2 * heads and heads % 4 == 0 and 2 * span == 5 * BLOCK:
+            body = functools.partial(on_chip_pair, seq_count, head_devices)
+        return jax.shard_map(
+            body,
+            mesh=mesh,
+            in_specs=(rows, rows, rows, rows, P()),
+            out_specs=(rows, rows, rows),
+            check_vma=False,
+        )(query, key, value, grad_out, rand_blocks)
+
+    return run

time: 639 us -> 160 us (0.25); the launches traced: 629 us -> 160 us
  local copies, waits for them, and re-layouts: 202 us -> 8.24 us
  waiting for transfers between devices: 295 us -> 104 us
  matrix products: 35.6 us -> 0 us
  starting transfers between devices: 50.8 us -> 21.5 us
  other arithmetic: 31.1 us -> 5.53 us
  Pallas kernels: 0 us -> 19.5 us
  between operations: 14.9 us -> 0.7 us
    ppermute x4 -> x2, waiting for transfers between devices: 202 us -> 0.01 us  [the longest x1 0.01 us: on_chip_pair(): part = lax.ppermute(dsib, 'head', swap)]
    another operation x14 -> x2, local copies, waits for them, and re-layouts: 89.8 us -> 1.54 us  [spread(): jnp.stack([a.reshape(span, chunks, HD).transpose(1, 0, 2) for a in arrays...]
    all_to_all x9 -> x4, waiting for transfers between devices: 45.6 us -> 104 us  [the longest x2 60.1 us: spread(): lax.all_to_all(cut, both, split_axis=0, concat_axis=0, axis_index_groups=...]
    psum x2 -> x0, waiting for transfers between devices: 46.9 us -> none  [the longest x1 24.9 us: broadcast(): return lax.psum(block, axis)]
    dot_general x7 -> x0, matrix products: 35.6 us -> none  [the longest x1 8.68 us: on_device(): jnp.einsum('dcb,dcsxf->sbxf', chooser, arrived.reshape(seq_count, capacit...]
    slice x7 -> x0, local copies, waits for them, and re-layouts: 20.2 us -> none  [the longest x1 9.6 us: on_device(): slot_keys = gathered[0].reshape(per_dev, slots_total, BLOCK, head_count, HD)]
    pallas_call x0 -> x1, Pallas kernels: none -> 19.5 us  [on_chip_pair(): pl.pallas_call(functools.partial(attend_kernel, chunks), out_shape=(jax.S...]
    unnamed x30 -> x14, local copies, waits for them, and re-layouts: 20.1 us -> 3.61 us
  transfers between devices with their start and end apart: 15 -> 6, of which waited for: 10 -> 4; matrix products, arithmetic and copies ran while one was open for 12% -> 4% of each run, Pallas kernels for 0% -> 0%
where the time goes in v1:
time: 160 us
  waiting for transfers between devices  104 us (65%)
  starting transfers between devices  21.5 us (13%)
  Pallas kernels  19.5 us (12%)
  local copies, waits for them, and re-layouts  8.24 us (5%)
  other arithmetic  5.53 us (3%)
    all_to_all x2, waiting for transfers between devices, spread(): lax.all_to_all(cut, both, split_axis=0, concat_axis=0, axis_index_groups=...  60.1 us
    all_to_all x2, waiting for transfers between devices, collect(): lax.all_to_all(cut, both, split_axis=0, concat_axis=0, axis_index_groups=...  44.2 us
    pallas_call x1, Pallas kernels, on_chip_pair(): pl.pallas_call(functools.partial(attend_kernel, chunks), out_shape=(jax.S...  19.5 us
    all_to_all x2, starting transfers between devices, spread(): lax.all_to_all(cut, both, split_axis=0, concat_axis=0, axis_index_groups=...  11.9 us
    all_to_all x2, starting transfers between devices, collect(): lax.all_to_all(cut, both, split_axis=0, concat_axis=0, axis_index_groups=...  9.55 us
    unnamed x14, local copies, waits for them, and re-layouts  3.61 us
  transfers between devices with their start and end apart: 6, of which 4 were waited for; matrix products, arithmetic and copies ran while one was open for 4% of the time, Pallas kernels for 0%

profile of v1, /device:TPU:12, one launch (start us, length us, event | category | flops | bytes accessed | tf_op | source)
XLA Modules:
  0.0 159.7 jit_solution(2930962754037241565)
XLA Ops:
  0.6 0.0 copy-start
  0.6 1.1 copy-done
  1.7 1.3 bitcast_bitcast_fusion
  3.0 1.2 pad_maximum_fusion.1
  4.2 0.0 copy-start.3
  4.2 0.0 copy-start.4
  4.2 7.3 %all-to-all-start.1 = ((bf16[16,2,160,128]{3,2,1,0:T(8,128)(2,1)}), bf16[16,2,160,128]{3,2,1,0:T(8,128)(2,1)S(1)}, u32[]{:S(2)}, u32[]{:S(2)}) async-start(bf16[16,2,160,128]{3,2,1,0:T(8,128)(2,1)} %pad_maximum_fusion.1), calls=%async_computation.1 | async-start | bytes 2621440 | tf_op jit(solution)/shard_map/all_to_all | solution.py:365
  11.5 0.0 copy-done.3
  11.5 0.0 copy-done.4
  11.5 0.2 bitcast_bitcast_fusion.2
  11.8 1.2 pad_maximum_fusion
  13.0 0.0 copy-start.5
  13.0 30.0 %all-to-all-done.1.own_ref = bf16[16,2,160,128]{3,2,1,0:T(8,128)(2,1)S(1)} async-done(((bf16[16,2,160,128]{3,2,1,0:T(8,128)(2,1)}), bf16[16,2,160,128]{3,2,1,0:T(8,128)(2,1)S(1)}, u32[]{:S(2)}, u32[]{:S(2)}) %all-to-all-start.1) | async-done | bytes 1310752 | tf_op jit(solution)/shard_map/all_to_all | solution.py:365
  43.0 4.6 %all-to-all-start = ((bf16[16,2,160,128]{3,2,1,0:T(8,128)(2,1)}), bf16[16,2,160,128]{3,2,1,0:T(8,128)(2,1)S(1)}, u32[]{:S(2)}, u32[]{:S(2)}) async-start(bf16[16,2,160,128]{3,2,1,0:T(8,128)(2,1)} %pad_maximum_fusion), calls=%async_computation | async-start | bytes 2621440 | tf_op jit(solution)/shard_map/all_to_all | solution.py:365
  47.6 0.0 collective-permute-start
  47.6 0.0 copy-done.5
  47.6 0.1 copy.8
  47.7 0.2 reshape.34.rand_ref
  47.9 30.1 %all-to-all-done.qd_ref = bf16[16,2,160,128]{3,2,1,0:T(8,128)(2,1)S(1)} async-done(((bf16[16,2,160,128]{3,2,1,0:T(8,128)(2,1)}), bf16[16,2,160,128]{3,2,1,0:T(8,128)(2,1)S(1)}, u32[]{:S(2)}, u32[]{:S(2)}) %all-to-all-start) | async-done | bytes 1310752 | tf_op jit(solution)/shard_map/all_to_all | solution.py:365
  78.0 0.0 collective-permute-done.sib_ref
  78.0 19.5 %shard_map.76 = (bf16[16,160,128]{2,1,0:T(8,128)(2,1)S(1)}, f32[16,2,160,128]{3,2,1,0:T(8,128)S(1)}, bf16[16,2,160,128]{3,2,1,0:T(8,128)(2,1)}) custom-call(s32[1]{0:T(128)} %bitcast.core_ref, s32[240]{0:T(256)S(1)} %reshape.34.rand_ref, bf16[16,2,160,128]{3,2,1,0:T(8,128)(2,1)S(1)} %all-to-all-done.qd_ref, ...), custom_call_target="tpu_custom_call" | custom-call | tf_op jit(solution)/shard_map/pallas_call | solution.py:375
  97.4 0.0 copy-start.1
  97.4 1.5 copy-done.1
  98.9 0.0 copy-start.2
  98.9 0.8 copy-done.2
  99.8 0.0 collective-permute-start.1
  99.8 4.4 %all-to-all-start.2 = ((bf16[16,160,128]{2,1,0:T(8,128)(2,1)}), bf16[16,160,128]{2,1,0:T(8,128)(2,1)S(1)}, u32[]{:S(2)}, u32[]{:S(2)}) async-start(bf16[16,160,128]{2,1,0:T(8,128)(2,1)} %copy-done.2), calls=%async_computation.2 | async-start | bytes 1310720 | tf_op jit(solution)/shard_map/all_to_all | solution.py:396
  104.2 0.0 collective-permute-done.1
  104.2 3.1 %add_convert_fusion = bf16[16,2,160,128]{3,2,1,0:T(8,128)(2,1)} fusion(f32[16,2,160,128]{3,2,1,0:T(8,128)} %copy-done.1, bf16[16,2,160,128]{3,2,1,0:T(8,128)(2,1)S(1)} %collective-permute-done.1), kind=kLoop, calls=%fused_computation | loop fusion | flops 1966080 | bytes 5242880 | tf_op jit(solution)/shard_map/convert_element_type | solution.py:393
  107.4 14.3 %all-to-all-done.2 = bf16[16,160,128]{2,1,0:T(8,128)(2,1)S(1)} async-done(((bf16[16,160,128]{2,1,0:T(8,128)(2,1)}), bf16[16,160,128]{2,1,0:T(8,128)(2,1)S(1)}, u32[]{:S(2)}, u32[]{:S(2)}) %all-to-all-start.2) | async-done | bytes 655392 | tf_op jit(solution)/shard_map/all_to_all | solution.py:396
  121.7 5.1 %all-to-all-start.3 = ((bf16[16,2,160,128]{3,2,1,0:T(8,128)(2,1)}), bf16[16,2,160,128]{3,2,1,0:T(8,128)(2,1)S(1)}, u32[]{:S(2)}, u32[]{:S(2)}) async-start(bf16[16,2,160,128]{3,2,1,0:T(8,128)(2,1)} %add_convert_fusion), calls=%async_computation.3 | async-start | bytes 2621440 | tf_op jit(solution)/shard_map/all_to_all | solution.py:396
  126.8 0.9 copy_bitcast_fusion.2
  127.7 29.9 %all-to-all-done.3 = bf16[16,2,160,128]{3,2,1,0:T(8,128)(2,1)S(1)} async-done(((bf16[16,2,160,128]{3,2,1,0:T(8,128)(2,1)}), bf16[16,2,160,128]{3,2,1,0:T(8,128)(2,1)S(1)}, u32[]{:S(2)}, u32[]{:S(2)}) %all-to-all-start.3) | async-done | bytes 1310752 | tf_op jit(solution)/shard_map/all_to_all | solution.py:396
  157.5 0.1 slice_bitcast_fusion
  157.6 1.0 copy.30
  158.6 1.0 copy.31
Async XLA Ops:
  0.6 1.1 copy-start
  4.2 7.3 %copy-start.3 = (bf16[160,2048]{1,0:T(8,128)(2,1)S(1)}, bf16[160,2048]{1,0:T(8,128)(2,1)}, u32[]{:S(2)}) copy-start(bf16[160,2048]{1,0:T(8,128)(2,1)} %param.5) | copy-start | bytes 1966084
  4.2 7.3 %copy-start.4 = (bf16[160,2048]{1,0:T(8,128)(2,1)S(1)}, bf16[160,2048]{1,0:T(8,128)(2,1)}, u32[]{:S(2)}) copy-start(bf16[160,2048]{1,0:T(8,128)(2,1)} %param.8) | copy-start | bytes 1966084
  4.2 38.7 %all-to-all-start.1 = ((bf16[16,2,160,128]{3,2,1,0:T(8,128)(2,1)}), bf16[16,2,160,128]{3,2,1,0:T(8,128)(2,1)S(1)}, u32[]{:S(2)}, u32[]{:S(2)}) async-start(bf16[16,2,160,128]{3,2,1,0:T(8,128)(2,1)} %pad_maximum_fusion.1), calls=%async_computation.1 | async-start | bytes 2621440 | tf_op jit(solution)/shard_map/all_to_all | solution.py:365
  13.0 34.6 %copy-start.5 = (s32[80,3]{0,1:T(4,128)S(1)}, s32[80,3]{0,1:T(4,128)}, u32[]{:S(2)}) copy-start(s32[80,3]{0,1:T(4,128)} %param.9) | copy-start | bytes 2884
  43.0 35.0 %all-to-all-start = ((bf16[16,2,160,128]{3,2,1,0:T(8,128)(2,1)}), bf16[16,2,160,128]{3,2,1,0:T(8,128)(2,1)S(1)}, u32[]{:S(2)}, u32[]{:S(2)}) async-start(bf16[16,2,160,128]{3,2,1,0:T(8,128)(2,1)} %pad_maximum_fusion), calls=%async_computation | async-start | bytes 2621440 | tf_op jit(solution)/shard_map/all_to_all | solution.py:365
  47.6 30.4 %collective-permute-start = (bf16[16,2,160,128]{3,2,1,0:T(8,128)(2,1)S(1)}, bf16[16,2,160,128]{3,2,1,0:T(8,128)(2,1)}, u32[]{:S(2)}, u32[]{:S(2)}) collective-permute-start(bf16[16,2,160,128]{3,2,1,0:T(8,128)(2,1)S(1)} %all-to-all-done.1.own_ref), channel_id=1, source_target_pairs={{0,1},{1,0},{2,3},{3,2},{4,5},{5,4},{6,7},{7,6},{8,9},{9,8},{10,11... | collective-permute-start | bytes 3932168 | tf_op jit(solution)/shard_map/ppermute | solution.py:371
  97.4 1.5 copy-start.1
  98.9 0.8 copy-start.2
  99.8 4.4 %collective-permute-start.1 = (bf16[16,2,160,128]{3,2,1,0:T(8,128)(2,1)}, bf16[16,2,160,128]{3,2,1,0:T(8,128)(2,1)S(1)}, u32[]{:S(2)}, u32[]{:S(2)}) collective-permute-start(bf16[16,2,160,128]{3,2,1,0:T(8,128)(2,1)} %get-tuple-element.8), channel_id=1, source_target_pairs={{0,1},{1,0},{2,3},{3,2},{4,5},{5,4},{6,7},{7,6},{8,9},{9,8},{10,11... | collective-permute-start | bytes 3932168 | tf_op jit(solution)/shard_map/ppermute | solution.py:392
  99.8 21.9 %all-to-all-start.2 = ((bf16[16,160,128]{2,1,0:T(8,128)(2,1)}), bf16[16,160,128]{2,1,0:T(8,128)(2,1)S(1)}, u32[]{:S(2)}, u32[]{:S(2)}) async-start(bf16[16,160,128]{2,1,0:T(8,128)(2,1)} %copy-done.2), calls=%async_computation.2 | async-start | bytes 1310720 | tf_op jit(solution)/shard_map/all_to_all | solution.py:396
  121.7 35.9 %all-to-all-start.3 = ((bf16[16,2,160,128]{3,2,1,0:T(8,128)(2,1)}), bf16[16,2,160,128]{3,2,1,0:T(8,128)(2,1)S(1)}, u32[]{:S(2)}, u32[]{:S(2)}) async-start(bf16[16,2,160,128]{3,2,1,0:T(8,128)(2,1)} %add_convert_fusion), calls=%async_computation.3 | async-start | bytes 2621440 | tf_op jit(solution)/shard_map/all_to_all | solution.py:396

commit v2 on v1

--- a/solution.py
+++ b/solution.py
@@ -278,23 +278,21 @@
         start += rows
 
 
-def attend_kernel(chunks, core_ref, rand_ref, qd_ref, own_ref, sib_ref, dq_ref, down_ref, dsib_ref,
-                  kf, vf, dkf, dvf):
-    span = qd_ref.shape[2]
-    half = BLOCK // 2
+def rows_at(g, which, span):
+    return pl.ds(pl.multiple_of(g * 2 * span + which * span, BLOCK // 2), span)
+
+
+def whole_kernel(chunks, span, core_ref, rand_ref, in_ref, sib_ref, dq_ref, kf, vf, dkf, dvf):
     per_pair = 2 * span // BLOCK
-    block_count = chunks * per_pair
     core = core_ref[0]
-
-    def rows_at(g, which):
-        return pl.ds(pl.multiple_of(g * 2 * span + which * span, half), span)
+    many = 2 * BLOCK
 
     def lay(g, carry):
-        mine, other = rows_at(g, core), rows_at(g, 1 - core)
-        kf[mine, :] = own_ref[g, 0]
-        vf[mine, :] = own_ref[g, 1]
-        kf[other, :] = sib_ref[g, 0]
-        vf[other, :] = sib_ref[g, 1]
+        mine, other = rows_at(g, core, span), rows_at(g, 1 - core, span)
+        kf[mine, :] = in_ref[g, :span]
+        vf[mine, :] = in_ref[g, span : 2 * span]
+        kf[other, :] = sib_ref[g, :span]
+        vf[other, :] = sib_ref[g, span:]
         zeros = jnp.zeros((span, HD), jnp.float32)
         for ref in (dkf, dvf):
             ref[mine, :] = zeros
@@ -303,49 +301,62 @@
 
     lax.fori_loop(0, chunks, lay, 0)
 
-    def run(units):
+    def put(at, rows, values):
+        dq_ref[at[0], at[1] : at[1] + rows] = values
+
+    def whole_blocks(g, carry):
+        q_at, do_at = 2 * span, 2 * span + many
         attend_units(
-            [(first, rows, j) for first, rows, j in units],
-            block_count,
+            [((g, i * BLOCK), BLOCK, g * per_pair + core * 3 + i) for i in range(2)],
+            chunks * per_pair,
             lambda j, r: rand_ref[j * R + r],
-            lambda at, rows: qd_ref[at[0], 0, pl.ds(pl.multiple_of(at[1], half), rows), :],
-            lambda at, rows: qd_ref[at[0], 1, pl.ds(pl.multiple_of(at[1], half), rows), :],
-            kf, vf, dkf, dvf,
-            put,
-        )
+            lambda at, rows: in_ref[at[0], q_at + at[1] : q_at + at[1] + rows],
+            lambda at, rows: in_ref[at[0], do_at + at[1] : do_at + at[1] + rows],
+            kf, vf, dkf, dvf, put,
+        )
+        return carry
+
+    lax.fori_loop(0, chunks, whole_blocks, 0)
+
+
+def half_kernel(chunks, span, core_ref, rand_ref, in_ref, kf, vf, dk_ref, dv_ref,
+                dq_ref, down_ref, dsib_ref, dkf, dvf):
+    per_pair = 2 * span // BLOCK
+    core = core_ref[0]
+    half = BLOCK // 2
+
+    def lay(g, carry):
+        for which in range(2):
+            rows = rows_at(g, which, span)
+            dkf[rows, :] = dk_ref[rows, :]
+            dvf[rows, :] = dv_ref[rows, :]
+        return carry
+
+    lax.fori_loop(0, chunks, lay, 0)
 
     def put(at, rows, values):
-        dq_ref[at[0], pl.ds(pl.multiple_of(at[1], half), rows), :] = values
-
-    def whole_blocks(g, carry):
-        run(
-            [
-                ((g, core * half + i * BLOCK), BLOCK, g * per_pair + core * 3 + i)
-                for i in range(2)
-            ]
+        dq_ref[at] = values
+
+    def half_blocks(t, carry):
+        attend_units(
+            [(t * 4 + i, half, (t * 4 + i) * per_pair + 2) for i in range(4)],
+            chunks * per_pair,
+            lambda j, r: rand_ref[j * R + r],
+            lambda at, rows: in_ref[at, :rows],
+            lambda at, rows: in_ref[at, rows:],
+            kf, vf, dkf, dvf, put,
         )
         return carry
 
-    lax.fori_loop(0, chunks, whole_blocks, 0)
-
-    def half_blocks(t, carry):
-        run(
-            [
-                ((t * 4 + i, (1 - core) * 2 * BLOCK), half, (t * 4 + i) * per_pair + 2)
-                for i in range(4)
-            ]
-        )
-        return carry
-
     lax.fori_loop(0, chunks // 4, half_blocks, 0)
 
     def hand_over(g, carry):
-        mine, other = rows_at(g, core), rows_at(g, 1 - core)
+        mine, other = rows_at(g, core, span), rows_at(g, 1 - core, span)
         scale = HD ** (-0.5)
-        down_ref[g, 0] = dkf[mine, :] * scale
-        down_ref[g, 1] = dvf[mine, :]
-        dsib_ref[g, 0] = (dkf[other, :] * scale).astype(jnp.bfloat16)
-        dsib_ref[g, 1] = dvf[other, :].astype(jnp.bfloat16)
+        down_ref[g, :span] = dkf[mine, :] * scale
+        down_ref[g, span:] = dvf[mine, :]
+        dsib_ref[g, :span] = (dkf[other, :] * scale).astype(jnp.bfloat16)
+        dsib_ref[g, span:] = dvf[other, :].astype(jnp.bfloat16)
         return carry
 
     lax.fori_loop(0, chunks, hand_over, 0)
@@ -358,51 +369,71 @@
     groups = [[i for i in range(count) if i % 2 == core] for core in range(2)]
     swap = [(i, i ^ 1) for i in range(head_devices)]
     span = query.shape[0]
+    half, many = BLOCK // 2, 2 * BLOCK
     core = lax.rem(lax.axis_index("head"), 2)
 
-    def spread(*arrays):
-        cut = jnp.stack([a.reshape(span, chunks, HD).transpose(1, 0, 2) for a in arrays], axis=1)
+    def exchange(cut):
         return lax.all_to_all(
             cut, both, split_axis=0, concat_axis=0, axis_index_groups=groups, tiled=True
         )
 
-    own = spread(key, value)
-    rows = spread(query, grad_out)
-    sib = lax.ppermute(own, "head", swap)
+    def spread(*arrays):
+        rows = jnp.concatenate(arrays, axis=0)
+        return exchange(rows.reshape(rows.shape[0], chunks, HD).transpose(1, 0, 2))
+
+    def wholes(a):
+        return lax.dynamic_slice_in_dim(a, core * half, many, axis=0)
+
+    def halves(a):
+        return lax.dynamic_slice_in_dim(a, (1 - core) * many, half, axis=0)
+
+    first = spread(key, value, wholes(query), wholes(grad_out))
+    second = spread(halves(query), halves(grad_out))
+    sib = lax.ppermute(first[:, : 2 * span], "head", swap)
     vmem = pl.BlockSpec(memory_space=pltpu.VMEM)
     smem = pl.BlockSpec(memory_space=pltpu.SMEM)
     total = chunks * 2 * span
-    dq, down, dsib = pl.pallas_call(
-        functools.partial(attend_kernel, chunks),
+    held = jax.ShapeDtypeStruct((total, HD), jnp.bfloat16)
+    sums = jax.ShapeDtypeStruct((total, HD), jnp.float32)
+    place, table = core.reshape(1), rand_blocks.reshape(-1)
+    params = pltpu.CompilerParams(vmem_limit_bytes=40 * 2**20)
+    dq_whole, kf, vf, dkf, dvf = pl.pallas_call(
+        functools.partial(whole_kernel, chunks, span),
+        out_shape=(jax.ShapeDtypeStruct((chunks, many, HD), jnp.bfloat16), held, held, sums, sums),
+        in_specs=[smem, smem, vmem, vmem],
+        out_specs=(vmem,) * 5,
+        compiler_params=params,
+        cost_estimate=pl.CostEstimate(flops=14 * 10**9, bytes_accessed=12 * 10**6, transcendentals=0),
+    )(place, table, first, sib)
+    got_whole = exchange(dq_whole)
+    dq_half, down, dsib = pl.pallas_call(
+        functools.partial(half_kernel, chunks, span),
         out_shape=(
-            jax.ShapeDtypeStruct((chunks, span, HD), jnp.bfloat16),
-            jax.ShapeDtypeStruct((chunks, 2, span, HD), jnp.float32),
-            jax.ShapeDtypeStruct((chunks, 2, span, HD), jnp.bfloat16),
+            jax.ShapeDtypeStruct((chunks, half, HD), jnp.bfloat16),
+            jax.ShapeDtypeStruct((chunks, 2 * span, HD), jnp.float32),
+            jax.ShapeDtypeStruct((chunks, 2 * span, HD), jnp.bfloat16),
         ),
-        in_specs=[smem, smem, vmem, vmem, vmem],
-        out_specs=(vmem, vmem, vmem),
-        scratch_shapes=[
-            pltpu.VMEM((total, HD), jnp.bfloat16),
-            pltpu.VMEM((total, HD), jnp.bfloat16),
-            pltpu.VMEM((total, HD), jnp.float32),
-            pltpu.VMEM((total, HD), jnp.float32),
-        ],
-        compiler_params=pltpu.CompilerParams(vmem_limit_bytes=40 * 2**20),
-    )(core.reshape(1), rand_blocks.reshape(-1), rows, own, sib)
+        in_specs=[smem, smem] + [vmem] * 5,
+        out_specs=(vmem,) * 3,
+        scratch_shapes=[pltpu.VMEM((total, HD), jnp.float32)] * 2,
+        compiler_params=params,
+        cost_estimate=pl.CostEstimate(flops=6 * 10**9, bytes_accessed=12 * 10**6, transcendentals=0),
+    )(place, table, second, kf, vf, dkf, dvf)
+    dsib, got_whole = lax.optimization_barrier((dsib, got_whole))
     part = lax.ppermute(dsib, "head", swap)
     summed = (down + part.astype(jnp.float32)).astype(jnp.bfloat16)
-
-    def collect(cut):
-        return lax.all_to_all(
-            cut, both, split_axis=0, concat_axis=0, axis_index_groups=groups, tiled=True
-        )
+    last = exchange(jnp.concatenate([summed, dq_half], axis=1))
 
     def flat(cut):
-        return cut.transpose(1, 0, 2).reshape(span, chunks * HD)
-
-    dq = flat(collect(dq))
-    both_grads = collect(summed)
-    return dq, flat(both_grads[:, 0]), flat(both_grads[:, 1])
+        return cut.transpose(1, 0, 2).reshape(cut.shape[1], chunks * HD)
+
+    got_half = last[:, 2 * span :]
+    dq = jnp.where(
+        core == 0,
+        jnp.concatenate([got_whole, got_half], axis=1),
+        jnp.concatenate([got_half, got_whole], axis=1),
+    )
+    return flat(dq), flat(last[:, :span]), flat(last[:, span : 2 * span])
 
 
 def solution(mesh):

time: 160 us -> 161 us (level)
  waiting for transfers between devices: 104 us -> 39.1 us
  blocking collectives: 0 us -> 60.2 us
  local copies, waits for them, and re-layouts: 8.24 us -> 18.5 us
  starting transfers between devices: 21.5 us -> 17.7 us
  other arithmetic: 5.53 us -> 3.8 us
    all_to_all x4 -> x3, waiting for transfers between devices: 104 us -> 35.9 us  [exchange(): lax.all_to_all(cut, both, split_axis=0, concat_axis=0, axis_index_groups=...]
    all_to_all x0 -> x1, blocking collectives: none -> 60.2 us  [exchange(): lax.all_to_all(cut, both, split_axis=0, concat_axis=0, axis_index_groups=...]
    unnamed x14 -> x26, local copies, waits for them, and re-layouts: 3.61 us -> 12.8 us
    all_to_all x4 -> x3, starting transfers between devices: 21.5 us -> 17.7 us  [exchange(): lax.all_to_all(cut, both, split_axis=0, concat_axis=0, axis_index_groups=...]
    ppermute x1, waiting for transfers between devices: 0.01 us -> 3.24 us  [on_chip_pair(): part = lax.ppermute(dsib, 'head', swap)]
    convert_element_type x1, other arithmetic: 3.14 us -> 0.37 us  [on_chip_pair(): summed = (down + part.astype(jnp.float32)).astype(jnp.bfloat16)]
    another operation x2 -> x0, other arithmetic: 2.39 us -> none  [spread(): jnp.stack([a.reshape(span, chunks, HD).transpose(1, 0, 2) for a in arrays...]
    dynamic_slice x0 -> x2, local copies, waits for them, and re-layouts: none -> 2.36 us  [the longest x1 1.37 us: wholes(): return lax.dynamic_slice_in_dim(a, core * half, many, axis=0)]
  transfers between devices with their start and end apart: 6 -> 5, of which waited for: 4 -> 3; matrix products, arithmetic and copies ran while one was open for 4% -> 1% of each run, Pallas kernels for 0% -> 13%
where the time goes in v2:
time: 161 us; the launch traced here: 160 us
  blocking collectives  60.2 us (37%)
  waiting for transfers between devices  39.1 us (24%)
  Pallas kernels  20.1 us (12%)
  local copies, waits for them, and re-layouts  18.5 us (11%)
  starting transfers between devices  17.7 us (11%)
  other arithmetic  3.8 us (2%)
    all_to_all x1, blocking collectives, exchange(): lax.all_to_all(cut, both, split_axis=0, concat_axis=0, axis_index_groups=...  60.2 us
    all_to_all x3, waiting for transfers between devices, exchange(): lax.all_to_all(cut, both, split_axis=0, concat_axis=0, axis_index_groups=...  35.9 us
    all_to_all x3, starting transfers between devices, exchange(): lax.all_to_all(cut, both, split_axis=0, concat_axis=0, axis_index_groups=...  17.7 us
    pallas_call x1, Pallas kernels, on_chip_pair(): pl.pallas_call(functools.partial(whole_kernel, chunks, span), out_shape=(...  14.4 us
    unnamed x26, local copies, waits for them, and re-layouts  12.8 us
    pallas_call x1, Pallas kernels, on_chip_pair(): pl.pallas_call(functools.partial(half_kernel, chunks, span), out_shape=(j...  5.71 us
    ppermute x1, waiting for transfers between devices, on_chip_pair(): part = lax.ppermute(dsib, 'head', swap)  3.24 us
  transfers between devices with their start and end apart: 5, of which 3 were waited for; matrix products, arithmetic and copies ran while one was open for 1% of the time, Pallas kernels for 13%

profile of v2, /device:TPU:12, one launch (start us, length us, event | category | flops | bytes accessed | tf_op | source)
XLA Modules:
  0.0 160.1 jit_solution(5522888317361596151)
XLA Ops:
  0.6 0.0 copy-start.10
  0.6 0.0 copy-start.9
  0.7 1.4 constant_dynamic-slice_fusion
  2.0 0.0 copy-done.10
  2.0 0.2 copy-done.9
  2.2 0.5 bitcast_bitcast_fusion
  2.7 60.2 %all_to_all.20.in_ref = bf16[16,576,128]{2,1,0:T(8,128)(2,1)S(1)} all-to-all(bf16[16,576,128]{2,1,0:T(8,128)(2,1)S(1)} %bitcast_bitcast_fusion), channel_id=1, replica_groups={{0,2,4,6,8,10,12,14,16,18,20,22,24,26,28,30},{1,3,5,7,9,11,13,15,17,19,..., dimensions={0} | all-to-all | bytes 4718592 | tf_op jit(solution)/shard_map/all_to_all | solution.py:376
  62.9 0.0 copy-start.11
  62.9 1.2 slice.16
  64.1 0.0 collective-permute-start
  64.1 1.0 constant_dynamic-slice_fusion.2
  65.1 0.8 bitcast_bitcast_fusion.1
  65.8 5.2 %all-to-all-start = ((bf16[16,64,128]{2,1,0:T(8,128)(2,1)}), bf16[16,64,128]{2,1,0:T(8,128)(2,1)S(1)}, u32[]{:S(2)}, u32[]{:S(2)}) async-start(bf16[16,64,128]{2,1,0:T(8,128)(2,1)} %bitcast_bitcast_fusion.1), calls=%async_computation | async-start | bytes 524288 | tf_op jit(solution)/shard_map/all_to_all | solution.py:376
  71.0 0.0 copy-done.11
  71.0 0.1 copy.8
  71.1 0.2 reshape.28.rand_ref
  71.3 0.0 collective-permute-done.sib_ref
  71.3 14.4 %shard_map.76 = (bf16[16,128,128]{2,1,0:T(8,128)(2,1)}, bf16[5120,128]{1,0:T(8,128)(2,1)S(1)}, bf16[5120,128]{1,0:T(8,128)(2,1)S(1)}, f32[5120,128]{1,0:T(8,128)S(1)}, f32[5120,128]{1,0:T(8,128)S(1)}) custom-call(s32[1]{0:T(128)} %bitcast.core_ref, s32[240]{0:T(256)S(1)} %reshape.28.rand_ref, bf16[16,576,128]{2,1,0:T(8,128)(2,1)S(1)} %all_to_all.20.in_ref, ...), custom_call_target="tpu_custom_call" | custom-call | flops 14000000000 | bytes 12000000 | tf_op jit(solution)/shard_map/pallas_call | solution.py:400
  85.7 0.0 copy-start.1
  85.7 1.5 copy-done.1
  87.2 0.0 copy-start.3
  87.2 1.6 copy-done.3
  88.8 0.0 copy-start.5
  88.8 1.1 copy-done.5
  89.9 0.0 copy-start.7
  89.9 1.0 copy-done.7
  90.9 0.0 all-to-all-done.in_ref
  90.9 7.0 %all-to-all-start.2 = ((bf16[16,128,128]{2,1,0:T(8,128)(2,1)}), bf16[16,128,128]{2,1,0:T(8,128)(2,1)S(1)}, u32[]{:S(2)}, u32[]{:S(2)}) async-start(bf16[16,128,128]{2,1,0:T(8,128)(2,1)} %get-tuple-element.18), calls=%async_computation.2 | async-start | bytes 1048576 | tf_op jit(solution)/shard_map/all_to_all | solution.py:376
  97.9 0.0 copy-start.2
  97.9 1.7 %copy-done.2 = f32[5120,128]{1,0:T(8,128)S(1)} copy-done((f32[5120,128]{1,0:T(8,128)S(1)}, f32[5120,128]{1,0:T(8,128)}, u32[]{:S(2)}) %copy-start.2) | copy-done | bytes 2621464
  99.7 0.0 copy-start.4
  99.7 1.7 %copy-done.4 = f32[5120,128]{1,0:T(8,128)S(1)} copy-done((f32[5120,128]{1,0:T(8,128)S(1)}, f32[5120,128]{1,0:T(8,128)}, u32[]{:S(2)}) %copy-start.4) | copy-done | bytes 2621464
  101.4 0.0 copy-start.6
  101.4 1.3 copy-done.6
  102.7 0.0 copy-start.8
  102.7 1.3 copy-done.8
  104.0 5.7 %shard_map.77 = (bf16[16,32,128]{2,1,0:T(8,128)(2,1)S(1)}, f32[16,320,128]{2,1,0:T(8,128)S(1)}, bf16[16,320,128]{2,1,0:T(8,128)(2,1)S(1)}) custom-call(s32[1]{0:T(128)} %bitcast.core_ref, s32[240]{0:T(256)S(1)} %reshape.28.rand_ref, bf16[16,64,128]{2,1,0:T(8,128)(2,1)S(1)} %all-to-all-done.in_ref, bf16[5120,128]{1,0:T(8,128)(2,1)S(1)} %copy-done.6, ...), custom_call_target="tpu_custom_call" | custom-call | flops 6000000000 | bytes 12000000 | tf_op jit(solution)/shard_map/pallas_call | solution.py:409
  109.7 0.0 copy-start
  109.8 1.1 copy-done
  110.8 1.4 all-to-all-done.2
  112.2 0.0 collective-permute-start.1
  112.2 3.2 %collective-permute-done.1 = bf16[16,320,128]{2,1,0:T(8,128)(2,1)S(1)} collective-permute-done((bf16[16,320,128]{2,1,0:T(8,128)(2,1)}, bf16[16,320,128]{2,1,0:T(8,128)(2,1)S(1)}, u32[]{:S(2)}, u32[]{:S(2)}) %collective-permute-start.1) | collective-permute-done | bytes 1310752 | tf_op jit(solution)/shard_map/ppermute | solution.py:423
  115.5 0.4 add_convert_fusion
  115.8 1.2 pad_maximum_fusion
  117.1 5.5 %all-to-all-start.3 = ((bf16[16,352,128]{2,1,0:T(8,128)(2,1)}), bf16[16,352,128]{2,1,0:T(8,128)(2,1)S(1)}, u32[]{:S(2)}, u32[]{:S(2)}) async-start(bf16[16,352,128]{2,1,0:T(8,128)(2,1)} %pad_maximum_fusion), calls=%async_computation.3 | async-start | bytes 2883584 | tf_op jit(solution)/shard_map/all_to_all | solution.py:376
  122.6 34.5 %all-to-all-done.3 = bf16[16,352,128]{2,1,0:T(8,128)(2,1)S(1)} async-done(((bf16[16,352,128]{2,1,0:T(8,128)(2,1)}), bf16[16,352,128]{2,1,0:T(8,128)(2,1)S(1)}, u32[]{:S(2)}, u32[]{:S(2)}) %all-to-all-start.3) | async-done | bytes 1441824 | tf_op jit(solution)/shard_map/all_to_all | solution.py:376
  157.0 0.1 slice_bitcast_fusion
  157.1 1.0 copy.24
  158.1 1.0 copy.25
  159.2 1.0 copy_bitcast_fusion.2
  (1 shorter events, 0.0 us)
Async XLA Ops:
  0.6 1.4 copy-start.10
  0.6 1.6 copy-start.9
  62.9 8.1 %copy-start.11 = (s32[80,3]{0,1:T(4,128)S(1)}, s32[80,3]{0,1:T(4,128)}, u32[]{:S(2)}) copy-start(s32[80,3]{0,1:T(4,128)} %param.9) | copy-start | bytes 2884
  64.1 7.2 %collective-permute-start = (bf16[16,320,128]{2,1,0:T(8,128)(2,1)}, bf16[16,320,128]{2,1,0:T(8,128)(2,1)}, u32[]{:S(2)}, u32[]{:S(2)}) collective-permute-start(bf16[16,320,128]{2,1,0:T(8,128)(2,1)} %slice.16), channel_id=1, source_target_pairs={{0,1},{1,0},{2,3},{3,2},{4,5},{5,4},{6,7},{7,6},{8,9},{9,8},{10,11... | collective-permute-start | bytes 3932168 | tf_op jit(solution)/shard_map/ppermute | solution.py:392
  65.8 25.1 %all-to-all-start = ((bf16[16,64,128]{2,1,0:T(8,128)(2,1)}), bf16[16,64,128]{2,1,0:T(8,128)(2,1)S(1)}, u32[]{:S(2)}, u32[]{:S(2)}) async-start(bf16[16,64,128]{2,1,0:T(8,128)(2,1)} %bitcast_bitcast_fusion.1), calls=%async_computation | async-start | bytes 524288 | tf_op jit(solution)/shard_map/all_to_all | solution.py:376
  85.7 1.5 copy-start.1
  87.2 1.6 copy-start.3
  88.8 1.1 copy-start.5
  89.9 1.1 copy-start.7
  90.9 21.3 %all-to-all-start.2 = ((bf16[16,128,128]{2,1,0:T(8,128)(2,1)}), bf16[16,128,128]{2,1,0:T(8,128)(2,1)S(1)}, u32[]{:S(2)}, u32[]{:S(2)}) async-start(bf16[16,128,128]{2,1,0:T(8,128)(2,1)} %get-tuple-element.18), calls=%async_computation.2 | async-start | bytes 1048576 | tf_op jit(solution)/shard_map/all_to_all | solution.py:376
  97.9 1.7 %copy-start.2 = (f32[5120,128]{1,0:T(8,128)S(1)}, f32[5120,128]{1,0:T(8,128)}, u32[]{:S(2)}) copy-start(f32[5120,128]{1,0:T(8,128)} %copy-done.1) | copy-start | bytes 7864324
  99.7 1.7 %copy-start.4 = (f32[5120,128]{1,0:T(8,128)S(1)}, f32[5120,128]{1,0:T(8,128)}, u32[]{:S(2)}) copy-start(f32[5120,128]{1,0:T(8,128)} %copy-done.3) | copy-start | bytes 7864324
  101.4 1.3 copy-start.6
  102.7 1.3 copy-start.8
  109.7 1.1 copy-start
  112.2 3.2 %collective-permute-start.1 = (bf16[16,320,128]{2,1,0:T(8,128)(2,1)}, bf16[16,320,128]{2,1,0:T(8,128)(2,1)S(1)}, u32[]{:S(2)}, u32[]{:S(2)}) collective-permute-start(bf16[16,320,128]{2,1,0:T(8,128)(2,1)} %copy-done), channel_id=1, source_target_pairs={{0,1},{1,0},{2,3},{3,2},{4,5},{5,4},{6,7},{7,6},{8,9},{9,8},{10,11... | collective-permute-start | bytes 3932168 | tf_op jit(solution)/shard_map/ppermute | solution.py:423
  117.1 40.0 %all-to-all-start.3 = ((bf16[16,352,128]{2,1,0:T(8,128)(2,1)}), bf16[16,352,128]{2,1,0:T(8,128)(2,1)S(1)}, u32[]{:S(2)}, u32[]{:S(2)}) async-start(bf16[16,352,128]{2,1,0:T(8,128)(2,1)} %pad_maximum_fusion), calls=%async_computation.3 | async-start | bytes 2883584 | tf_op jit(solution)/shard_map/all_to_all | solution.py:376

commit v3 on v2

--- a/solution.py
+++ b/solution.py
@@ -387,8 +387,10 @@
     def halves(a):
         return lax.dynamic_slice_in_dim(a, (1 - core) * many, half, axis=0)
 
-    first = spread(key, value, wholes(query), wholes(grad_out))
-    second = spread(halves(query), halves(grad_out))
+    first = spread(
+        key, value, wholes(query), wholes(grad_out), halves(query), halves(grad_out)
+    )
+    second = first[:, 2 * span + 2 * many :]
     sib = lax.ppermute(first[:, : 2 * span], "head", swap)
     vmem = pl.BlockSpec(memory_space=pltpu.VMEM)
     smem = pl.BlockSpec(memory_space=pltpu.SMEM)
@@ -405,7 +407,6 @@
         compiler_params=params,
         cost_estimate=pl.CostEstimate(flops=14 * 10**9, bytes_accessed=12 * 10**6, transcendentals=0),
     )(place, table, first, sib)
-    got_whole = exchange(dq_whole)
     dq_half, down, dsib = pl.pallas_call(
         functools.partial(half_kernel, chunks, span),
         out_shape=(
@@ -419,15 +420,14 @@
         compiler_params=params,
         cost_estimate=pl.CostEstimate(flops=6 * 10**9, bytes_accessed=12 * 10**6, transcendentals=0),
     )(place, table, second, kf, vf, dkf, dvf)
-    dsib, got_whole = lax.optimization_barrier((dsib, got_whole))
     part = lax.ppermute(dsib, "head", swap)
     summed = (down + part.astype(jnp.float32)).astype(jnp.bfloat16)
-    last = exchange(jnp.concatenate([summed, dq_half], axis=1))
+    last = exchange(jnp.concatenate([summed, dq_half, dq_whole], axis=1))
 
     def flat(cut):
         return cut.transpose(1, 0, 2).reshape(cut.shape[1], chunks * HD)
 
-    got_half = last[:, 2 * span :]
+    got_half, got_whole = last[:, 2 * span : 2 * span + half], last[:, 2 * span + half :]
     dq = jnp.where(
         core == 0,
         jnp.concatenate([got_whole, got_half], axis=1),

time: 161 us -> 166 us (1.031)
  waiting for transfers between devices: 39.1 us -> 51.8 us
  starting transfers between devices: 17.7 us -> 5.32 us
  blocking collectives: 60.2 us -> 66 us
  local copies, waits for them, and re-layouts: 18.5 us -> 20.3 us
  other arithmetic: 3.8 us -> 2.03 us
    all_to_all x3 -> x1, starting transfers between devices: 17.7 us -> 5.11 us  [exchange(): lax.all_to_all(cut, both, split_axis=0, concat_axis=0, axis_index_groups=...]
    all_to_all x3 -> x1, waiting for transfers between devices: 35.9 us -> 45.8 us  [exchange(): lax.all_to_all(cut, both, split_axis=0, concat_axis=0, axis_index_groups=...]
    concatenate x0 -> x1, local copies, waits for them, and re-layouts: none -> 6.04 us  [spread(): rows = jnp.concatenate(arrays, axis=0)]
    all_to_all x1, blocking collectives: 60.2 us -> 66 us  [exchange(): lax.all_to_all(cut, both, split_axis=0, concat_axis=0, axis_index_groups=...]
    unnamed x26 -> x15, local copies, waits for them, and re-layouts: 12.8 us -> 7.03 us
    ppermute x1, waiting for transfers between devices: 0.01 us -> 3.09 us  [on_chip_pair(): sib = lax.ppermute(first[:, :2 * span], 'head', swap)]
    reshape x0 -> x1, local copies, waits for them, and re-layouts: none -> 2.64 us  [spread(): return exchange(rows.reshape(rows.shape[0], chunks, HD).transpose(1, 0, 2))]
  transfers between devices with their start and end apart: 5 -> 3, of which waited for: 3 -> 3; matrix products, arithmetic and copies ran while one was open for 1% -> 0% of each run, Pallas kernels for 13% -> 0%
where the time goes in v3:
time: 166 us; the launch traced here: 165 us
  blocking collectives  66 us (40%)
  waiting for transfers between devices  51.8 us (31%)
  local copies, waits for them, and re-layouts  20.3 us (12%)
  Pallas kernels  19.3 us (12%)
  starting transfers between devices  5.32 us (3%)
  other arithmetic  2.03 us (1%)
    all_to_all x1, blocking collectives, exchange(): lax.all_to_all(cut, both, split_axis=0, concat_axis=0, axis_index_groups=...  66 us
    all_to_all x1, waiting for transfers between devices, exchange(): lax.all_to_all(cut, both, split_axis=0, concat_axis=0, axis_index_groups=...  45.8 us
    pallas_call x1, Pallas kernels, on_chip_pair(): pl.pallas_call(functools.partial(whole_kernel, chunks, span), out_shape=(...  13.6 us
    unnamed x15, local copies, waits for them, and re-layouts  7.03 us
    concatenate x1, local copies, waits for them, and re-layouts, spread(): rows = jnp.concatenate(arrays, axis=0)  6.04 us
    pallas_call x1, Pallas kernels, on_chip_pair(): pl.pallas_call(functools.partial(half_kernel, chunks, span), out_shape=(j...  5.7 us
    all_to_all x1, starting transfers between devices, exchange(): lax.all_to_all(cut, both, split_axis=0, concat_axis=0, axis_index_groups=...  5.11 us
  transfers between devices with their start and end apart: 3, of which 3 were waited for; matrix products, arithmetic and copies ran while one was open for 0% of the time, Pallas kernels for 0%

profile of v3, /device:TPU:12, one launch (start us, length us, event | category | flops | bytes accessed | tf_op | source)
XLA Modules:
  0.0 165.5 jit_solution(17842732662210757051)
XLA Ops:
  0.6 0.0 copy-start.2
  0.6 0.0 copy-start
  0.7 0.0 copy-start.1
  0.7 2.3 %copy.13 = bf16[160,2048]{0,1:T(8,128)(2,1)} copy(bf16[160,2048]{1,0:T(8,128)(2,1)} %param.6) | data formatting | bytes 1310720 | tf_op args[1]
  3.0 0.0 copy-done.2
  3.0 1.3 copy.14
  4.3 0.0 copy-done
  4.3 0.0 copy-done.1
  4.3 0.1 constant_dynamic-slice_fusion.2
  4.4 1.0 copy.19
  5.4 1.0 copy.20
  6.4 0.3 copy.21
  6.7 1.0 copy.22
  7.7 6.0 %concatenate.12 = bf16[640,2048]{0,1:T(8,128)(2,1)S(1)} concatenate(bf16[160,2048]{0,1:T(8,128)(2,1)} %copy.13, bf16[160,2048]{0,1:T(8,128)(2,1)} %copy.14, bf16[128,2048]{0,1:T(8,128)(2,1)} %copy.19, bf16[128,2048]{0,1:T(8,128)(2,1)} %copy.20, bf16[32,2048]{0,1:T(8,128)(2,1)S(1)} %copy.21, bf16[32,2048]{0,1:T(8,128)(2,1)} %copy.22), dimensions={0} | concatenate | bytes 5242880 | tf_op jit(solution)/shard_map/concatenate | solution.py:381
  13.8 2.6 %copy.15 = bf16[640,16,128]{2,0,1:T(8,128)(2,1)} copy(bf16[640,16,128]{0,2,1:T(8,128)(2,1)S(1)} %bitcast.21) | data formatting | bytes 5242880 | tf_op jit(solution)/shard_map/reshape | solution.py:382
  16.4 66.0 %all_to_all.10.in_ref = bf16[16,640,128]{2,1,0:T(8,128)(2,1)S(1)} all-to-all(bf16[16,640,128]{2,1,0:T(8,128)(2,1)} %bitcast.22), channel_id=1, replica_groups={{0,2,4,6,8,10,12,14,16,18,20,22,24,26,28,30},{1,3,5,7,9,11,13,15,17,19,..., dimensions={0} | all-to-all | bytes 5242880 | tf_op jit(solution)/shard_map/all_to_all | solution.py:376
  82.4 0.0 copy-start.3
  82.4 1.2 slice.26
  83.6 0.0 collective-permute-start
  83.6 0.0 copy-done.3
  83.6 0.1 copy.8
  83.7 0.2 reshape.25.rand_ref
  83.9 3.1 %collective-permute-done.sib_ref = bf16[16,320,128]{2,1,0:T(8,128)(2,1)} collective-permute-done((bf16[16,320,128]{2,1,0:T(8,128)(2,1)}, bf16[16,320,128]{2,1,0:T(8,128)(2,1)}, u32[]{:S(2)}, u32[]{:S(2)}) %collective-permute-start) | collective-permute-done | bytes 1310752 | tf_op jit(solution)/shard_map/ppermute | solution.py:394
  87.0 13.6 %shard_map.76 = (bf16[16,128,128]{2,1,0:T(8,128)(2,1)S(1)}, bf16[5120,128]{1,0:T(8,128)(2,1)S(1)}, bf16[5120,128]{1,0:T(8,128)(2,1)S(1)}, f32[5120,128]{1,0:T(8,128)S(1)}, f32[5120,128]{1,0:T(8,128)S(1)}) custom-call(s32[1]{0:T(128)} %bitcast.core_ref, s32[240]{0:T(256)S(1)} %reshape.25.rand_ref, bf16[16,640,128]{2,1,0:T(8,128)(2,1)S(1)} %all_to_all.10.in_ref, ...), custom_call_target="tpu_custom_call" | custom-call | flops 14000000000 | bytes 12000000 | tf_op jit(solution)/shard_map/pallas_call | solution.py:402
  100.6 5.7 %shard_map.77 = (bf16[16,32,128]{2,1,0:T(8,128)(2,1)S(1)}, f32[16,320,128]{2,1,0:T(8,128)S(1)}, bf16[16,320,128]{2,1,0:T(8,128)(2,1)S(1)}) custom-call(s32[1]{0:T(128)} %bitcast.core_ref, s32[240]{0:T(256)S(1)} %reshape.25.rand_ref, bf16[16,64,128]{2,1,0:T(8,128)(2,1)S(1)} %slice.25.in_ref, bf16[5120,128]{1,0:T(8,128)(2,1)S(1)} %get-tuple-element.11.kf, ...), custom_call_target="tpu_custom_call" | custom-call | flops 6000000000 | bytes 12000000 | tf_op jit(solution)/shard_map/pallas_call | solution.py:410
  106.3 0.2 collective-permute-start.1
  106.5 2.9 %collective-permute-done.1 = bf16[16,320,128]{2,1,0:T(8,128)(2,1)S(1)} collective-permute-done((bf16[16,320,128]{2,1,0:T(8,128)(2,1)S(1)}, bf16[16,320,128]{2,1,0:T(8,128)(2,1)S(1)}, u32[]{:S(2)}, u32[]{:S(2)}) %collective-permute-start.1) | collective-permute-done | bytes 1310752 | tf_op jit(solution)/shard_map/ppermute | solution.py:423
  109.4 0.4 add_convert_fusion
  109.8 1.4 pad_maximum_fusion
  111.2 5.1 %all-to-all-start.1 = ((bf16[16,480,128]{2,1,0:T(8,128)(2,1)}), bf16[16,480,128]{2,1,0:T(8,128)(2,1)S(1)}, u32[]{:S(2)}, u32[]{:S(2)}) async-start(bf16[16,480,128]{2,1,0:T(8,128)(2,1)} %pad_maximum_fusion), calls=%async_computation.1 | async-start | bytes 3932160 | tf_op jit(solution)/shard_map/all_to_all | solution.py:376
  116.3 45.8 %all-to-all-done.1 = bf16[16,480,128]{2,1,0:T(8,128)(2,1)S(1)} async-done(((bf16[16,480,128]{2,1,0:T(8,128)(2,1)}), bf16[16,480,128]{2,1,0:T(8,128)(2,1)S(1)}, u32[]{:S(2)}, u32[]{:S(2)}) %all-to-all-start.1) | async-done | bytes 1966112 | tf_op jit(solution)/shard_map/all_to_all | solution.py:376
  162.2 0.2 slice_bitcast_fusion
  162.4 1.0 copy.31
  163.4 1.0 copy.30
  164.5 1.0 copy.29
  (4 shorter events, 0.1 us)
Async XLA Ops:
  0.6 2.4 %copy-start.2 = (bf16[160,2048]{1,0:T(8,128)(2,1)S(1)}, bf16[160,2048]{1,0:T(8,128)(2,1)}, u32[]{:S(2)}) copy-start(bf16[160,2048]{1,0:T(8,128)(2,1)} %param.7) | copy-start | bytes 1966084
  0.6 3.7 %copy-start = (bf16[160,2048]{1,0:T(8,128)(2,1)S(1)}, bf16[160,2048]{1,0:T(8,128)(2,1)}, u32[]{:S(2)}) copy-start(bf16[160,2048]{1,0:T(8,128)(2,1)} %param.8) | copy-start | bytes 1966084
  0.7 3.7 %copy-start.1 = (bf16[160,2048]{1,0:T(8,128)(2,1)S(1)}, bf16[160,2048]{1,0:T(8,128)(2,1)}, u32[]{:S(2)}) copy-start(bf16[160,2048]{1,0:T(8,128)(2,1)} %param.5) | copy-start | bytes 1966084
  82.4 1.2 copy-start.3
  83.6 3.4 %collective-permute-start = (bf16[16,320,128]{2,1,0:T(8,128)(2,1)}, bf16[16,320,128]{2,1,0:T(8,128)(2,1)}, u32[]{:S(2)}, u32[]{:S(2)}) collective-permute-start(bf16[16,320,128]{2,1,0:T(8,128)(2,1)} %slice.26), channel_id=1, source_target_pairs={{0,1},{1,0},{2,3},{3,2},{4,5},{5,4},{6,7},{7,6},{8,9},{9,8},{10,11... | collective-permute-start | bytes 3932168 | tf_op jit(solution)/shard_map/ppermute | solution.py:394
  106.3 3.1 %collective-permute-start.1 = (bf16[16,320,128]{2,1,0:T(8,128)(2,1)S(1)}, bf16[16,320,128]{2,1,0:T(8,128)(2,1)S(1)}, u32[]{:S(2)}, u32[]{:S(2)}) collective-permute-start(bf16[16,320,128]{2,1,0:T(8,128)(2,1)S(1)} %get-tuple-element.16), channel_id=1, source_target_pairs={{0,1},{1,0},{2,3},{3,2},{4,5},{5,4},{6,7},{7,6},{8,9},{9,8},{10,11... | collective-permute-start | bytes 3932168 | tf_op jit(solution)/shard_map/ppermute | solution.py:423
  111.2 50.9 %all-to-all-start.1 = ((bf16[16,480,128]{2,1,0:T(8,128)(2,1)}), bf16[16,480,128]{2,1,0:T(8,128)(2,1)S(1)}, u32[]{:S(2)}, u32[]{:S(2)}) async-start(bf16[16,480,128]{2,1,0:T(8,128)(2,1)} %pad_maximum_fusion), calls=%async_computation.1 | async-start | bytes 3932160 | tf_op jit(solution)/shard_map/all_to_all | solution.py:376
